TPU v7x, 256 devices: a whole 4x4x8 slice. The times are simulated.
256 devices in a mesh: shot: 64 (over y, z_hi, x), gz: 4 (over z_lo, core).
Axes of the slice: x: 4, y: 4, z: 8 (z_hi: 4, z_lo: 2; z = z_hi * 2 + z_lo), core: 2. Of those that a mesh axis runs over, the one named last changes fastest.
Arguments:
- squared_courant: float32 [128, 512, 128], P('gz', 'shot'), may hold values from 0.05 to 0.19
- window_offset: int32 [64], P('shot'), may hold values from -2 to 2, as said below
- field_last: float32 [64, 128, 64, 128], P('shot', 'gz'), may hold values from -4 to 4
- field_after: float32 [64, 128, 64, 128], P('shot', 'gz'), may hold values from -4 to 4
- adjoint_last: float32 [64, 128, 64, 128], P('shot', 'gz'), may hold values from -4 to 4
- adjoint_after: float32 [64, 128, 64, 128], P('shot', 'gz'), may hold values from -4 to 4
- source_place: int32 [64, 3], P('shot'), may hold values from 0 to 127, as said below
- source_wavelet: float32 [64, 4], P('shot'), may hold values from -12 to 12
- receiver_place: int32 [64, 3, 128], P('shot'), may hold values from 0 to 127, as said below
- receiver_trace: float32 [64, 4, 128], P('shot'), may hold values from -6 to 6
Outputs:
- field_early: float32 [64, 128, 64, 128], P('shot', 'gz')
- adjoint_early: float32 [64, 128, 64, 128], P('shot', 'gz')
- model_gradient: float32 [128, 512, 128], P('gz', 'shot')
Inputs may be any that keep to these rules, and one draw needn't show every extreme that they name: `window_offset`: offsets of -2 and 2 both occur. `source_place`: column 0 is below 128, column 1 below 64, column 2 below 128. `receiver_place`: row 0 is below 128, row 1 below 64, row 2 below 128; receivers may share cells.
All inputs are finite; a program needn't handle non-finite values.
Results may differ from a plain program's by a relative error of at most 0.00002.
Values sent between devices are 32-bit elements; how exact they have to be, the bound alone decides.
A program may use at most 128 MiB of HBM per device.

v0:
```python
import functools
import math

import jax
import jax.numpy as jnp
import numpy as np
from jax import lax
from jax.experimental import pallas as pl
from jax.experimental.pallas import tpu as pltpu
from jax.sharding import PartitionSpec as P

WB = 8
SPREAD = 2
STEPS = 4
SPAN = WB + 2 * SPREAD
HALO = 4
CHUNK = 4
SCALE = 5040.0
CENTRE = -3.0 * 14350.0
SIDE = (8064.0, -1008.0, 128.0, -9.0)
MESH = pl.DeviceIdType.MESH


def banded(rows, cols, period):
    i = lax.broadcasted_iota(jnp.int32, (rows, cols), 0)
    j = lax.broadcasted_iota(jnp.int32, (rows, cols), 1)
    gap = jnp.abs(lax.rem(i, period) - lax.rem(j, period))
    band = jnp.zeros((rows, cols), jnp.float32)
    for k in range(1, 5):
        band = jnp.where(gap == k, SIDE[k - 1], band)
    return band.astype(jnp.bfloat16)


def in_two(values):
    high = values.astype(jnp.bfloat16)
    low = (values - high.astype(jnp.float32)).astype(jnp.bfloat16)
    return high, low


def kernel(
    offset_ref,
    spot_ref,
    wavelet_ref,
    receivers_ref,
    traces_ref,
    taper_ref,
    courant_ref,
    field_last,
    field_after,
    adjoint_last,
    adjoint_after,
    field_out,
    adjoint_out,
    gradient_out,
    fields,
    pieces,
    laps,
    model,
    imaging,
    shown,
    outgoing,
    arriving,
    gradient,
    hits,
    amounts,
    load_sem,
    halo_send,
    halo_recv,
    piece_send,
    piece_recv,
    back_send,
    back_recv,
):
    shot = lax.axis_index("shot")
    slab = lax.axis_index("gz")
    shots = lax.axis_size("shot")
    slabs = lax.axis_size("gz")
    depth, width, across = field_last.shape
    chunks = depth // CHUNK
    has = (slab > 0, slab < slabs - 1)
    beside = (jnp.maximum(slab - 1, 0), jnp.minimum(slab + 1, slabs - 1))

    def partner(k):
        return lax.rem(shot + k + shots, shots)

    loads = []
    for i, (buffer, which, source) in enumerate(
        ((0, 0, field_last), (0, 1, adjoint_last), (1, 0, field_after), (1, 1, adjoint_after))
    ):
        loads.append(pltpu.make_async_copy(source, fields.at[buffer, which, pl.ds(HALO, depth)], load_sem.at[i]))
    loads.append(pltpu.make_async_copy(courant_ref, pieces.at[SPREAD], load_sem.at[4]))
    for copy in loads:
        copy.start()

    blank = jnp.zeros((HALO, width, across), jnp.float32)
    for side, place in ((0, 0), (1, HALO + depth)):

        @pl.when(jnp.logical_not(has[side]))
        def _():
            for buffer in range(2):
                for which in range(2):
                    fields[buffer, which, pl.ds(place, HALO)] = blank

    barrier = pltpu.get_barrier_semaphore()
    for k in range(-(SPAN - SPREAD - 1), SPAN - SPREAD):
        if k != 0:
            pl.semaphore_signal(barrier, inc=1, device_id={"shot": partner(k)}, device_id_type=MESH)
    for side in range(2):

        @pl.when(has[side])
        def _():
            pl.semaphore_signal(barrier, inc=1, device_id={"gz": beside[side]}, device_id_type=MESH)

    beside_count = jnp.where(has[0], 1, 0) + jnp.where(has[1], 1, 0)
    pl.semaphore_wait(barrier, 2 * (SPAN - SPREAD - 1) + beside_count)

    def halo(turn, which, side):
        place = HALO if side == 0 else depth
        landing = HALO + depth if side == 0 else 0
        if turn == 0:
            source = (field_last, adjoint_last)[which].at[pl.ds(place - HALO, HALO)]
        else:
            source = fields.at[turn % 2, which, pl.ds(place, HALO)]
        return pltpu.make_async_remote_copy(
            src_ref=source,
            dst_ref=fields.at[turn % 2, which, pl.ds(landing, HALO)],
            send_sem=halo_send.at[turn, which, side],
            recv_sem=halo_recv.at[turn, which, side],
            device_id={"gz": beside[side]},
            device_id_type=MESH,
        )

    def halo_start(turn, which, side):
        @pl.when(has[side])
        def _():
            halo(turn, which, side).start()

    def halo_arrived(turn, which, side):
        @pl.when(has[side])
        def _():
            halo(turn, which, 1 - side).wait_recv()

    def halo_sent(turn, which, side):
        @pl.when(has[side])
        def _():
            halo(turn, which, side).wait_send()

    def piece_copy(j):
        return pltpu.make_async_remote_copy(
            src_ref=courant_ref,
            dst_ref=pieces.at[j],
            send_sem=piece_send.at[j],
            recv_sem=piece_recv.at[j],
            device_id={"shot": partner(SPREAD - j)},
            device_id_type=MESH,
        )

    def back_copy(j):
        return pltpu.make_async_remote_copy(
            src_ref=outgoing.at[j],
            dst_ref=arriving.at[j],
            send_sem=back_send.at[j],
            recv_sem=back_recv.at[j],
            device_id={"shot": partner(j - SPREAD)},
            device_id_type=MESH,
        )

    for which in range(2):
        for side in range(2):
            halo_start(0, which, side)
    others = [j for j in range(SPAN) if j != SPREAD]
    for j in others:
        piece_copy(j).start()

    offset = offset_ref[0]
    by_y = banded(2 * across, across, across)
    by_x = banded(width, 2 * width, width)
    row = lax.broadcasted_iota(jnp.int32, (width * CHUNK, across), 0)
    place = (receivers_ref[0:1, :] - slab * depth) * width + receivers_ref[1:2, :]

    def mark(c, _):
        start = pl.multiple_of(c * CHUNK * width, CHUNK * width)
        hits[pl.ds(start, CHUNK * width), :] = jnp.where(row + start == place, 1.0, 0.0).astype(jnp.bfloat16)
        return 0

    lax.fori_loop(0, chunks, mark, 0)
    along = lax.broadcasted_iota(jnp.int32, (across, across), 0) == receivers_ref[2:3, :]
    for step in range(STEPS):
        high, low = in_two(jnp.where(along, traces_ref[step : step + 1, :], 0.0))
        amounts[step, :, 0:across] = high
        amounts[step, :, across : 2 * across] = low
    spot = jnp.where(
        (lax.broadcasted_iota(jnp.int32, (width, across), 0) == spot_ref[1])
        & (lax.broadcasted_iota(jnp.int32, (width, across), 1) == spot_ref[2]),
        1.0,
        0.0,
    )
    spot_depth = spot_ref[0] - slab * depth
    shown[pl.ds(0, 4)] = jnp.zeros((4, depth, WB, across), jnp.float32)
    shown[pl.ds(12, 4)] = jnp.zeros((4, depth, WB, across), jnp.float32)

    def stencil(buffer, which, z0):
        centre = fields[buffer, which, pl.ds(z0 + HALO, CHUNK)]
        high, low = in_two(centre)
        rows = CHUNK * width
        left = jnp.concatenate([high.reshape(rows, across), low.reshape(rows, across)], axis=1)
        in_y = jnp.dot(left, by_y, preferred_element_type=jnp.float32)
        right = jnp.concatenate(
            [
                jnp.concatenate([high[c] for c in range(CHUNK)], axis=1),
                jnp.concatenate([low[c] for c in range(CHUNK)], axis=1),
            ],
            axis=0,
        )
        in_x = jnp.dot(by_x, right, preferred_element_type=jnp.float32)
        result = []
        for c in range(CHUNK):
            total = CENTRE * centre[c] + in_y[c * width : (c + 1) * width] + in_x[:, c * across : (c + 1) * across]
            for k in range(1, 5):
                above = fields[buffer, which, z0 + HALO + c + k]
                below = fields[buffer, which, z0 + HALO + c - k]
                total = total + SIDE[k - 1] * (above + below)
            result.append(total)
        return centre, result

    def injected(step, z0):
        start = pl.multiple_of(z0 * width, CHUNK * width)
        found = hits[pl.ds(start, CHUNK * width), :]
        return lax.dot_general(
            jnp.concatenate([found, found], axis=1),
            amounts[step],
            (((1,), (1,)), ((), ())),
            preferred_element_type=jnp.float32,
        )

    def advance(step, which, z0, centre, lap):
        later = 1 - step % 2
        if which == 1:
            added = injected(step, z0)
        for c in range(CHUNK):
            if which == 0:
                extra = spot * jnp.where(z0 + c == spot_depth, wavelet_ref[step], 0.0)
            else:
                extra = added[c * width : (c + 1) * width]
            fields[later, which, z0 + HALO + c] = (
                2.0 * centre[c] - fields[later, which, z0 + HALO + c] + model[z0 + c] * lap[c] + extra
            )

    def see(step, z0, lap):
        now = step % 2
        for c in range(CHUNK):
            seen = fields[now, 1, z0 + HALO + c] * lap[c]
            if step > 0:
                seen = imaging[z0 + c] + seen
            if step < STEPS - 1:
                imaging[z0 + c] = seen
            else:
                weighted = taper_ref[...] * seen
                for s in range(WB):
                    shown[4 + s, z0 + c] = weighted[s * WB : (s + 1) * WB]

    def first_part(which, z0):
        _, lap = stencil(0, which, z0)
        for c in range(CHUNK):
            laps[which, z0 + c] = lap[c]
        if which == 0:
            see(0, z0, lap)

    def second_part(which, z0):
        centre = fields[0, which, pl.ds(z0 + HALO, CHUNK)]
        advance(0, which, z0, centre, [laps[which, z0 + c] for c in range(CHUNK)])

    def whole(step, which, z0):
        centre, lap = stencil(step % 2, which, z0)
        if which == 0:
            see(step, z0, lap)
        advance(step, which, z0, centre, lap)

    def inner(body):
        def turn(c, _):
            body(pl.multiple_of(c * CHUNK, CHUNK))
            return 0

        lax.fori_loop(1, chunks - 1, turn, 0)

    ends = (0, depth - CHUNK)
    for copy in loads[:2]:
        copy.wait()
    for which in range(2):
        inner(functools.partial(first_part, which))
    for which in range(2):
        for side in range(2):
            halo_arrived(0, which, side)
            first_part(which, ends[side])
    for copy in loads[2:]:
        copy.wait()
    for j in others:
        piece_copy(j).wait_recv()
    for s in range(WB):
        model[:, s * WB : (s + 1) * WB, :] = pieces[offset + SPREAD + s] * (1.0 / SCALE)
    for which in range(2):
        for side in range(2):
            second_part(which, ends[side])
            halo_start(1, which, side)
    for which in range(2):
        inner(functools.partial(second_part, which))

    for step in range(1, STEPS):
        for which in range(2):
            for side in range(2):
                halo_arrived(step, which, side)
                if step > 1:
                    halo_sent(step - 1, which, side)
                whole(step, which, ends[side])
                if step < STEPS - 1:
                    halo_start(step + 1, which, side)
            inner(functools.partial(whole, step, which))
            if step == STEPS - 1 and which == 0:
                field_copy = pltpu.make_async_copy(fields.at[0, 0, pl.ds(HALO, depth)], field_out, load_sem.at[0])
                field_copy.start()
                for j in range(SPAN):
                    outgoing[j] = shown[j + 2 - offset]
                    if j != SPREAD:
                        back_copy(j).start()
    adjoint_copy = pltpu.make_async_copy(fields.at[0, 1, pl.ds(HALO, depth)], adjoint_out, load_sem.at[1])
    adjoint_copy.start()
    for which in range(2):
        for side in range(2):
            halo_sent(0, which, side)
            halo_sent(STEPS - 1, which, side)
    for j in others:
        piece_copy(j).wait_send()
    for j in others:
        back_copy(j).wait_recv()

    def add_up(c, _):
        total = outgoing[SPREAD, pl.ds(c * CHUNK, CHUNK)]
        for j in others:
            total = total + arriving[j, pl.ds(c * CHUNK, CHUNK)]
        gradient[pl.ds(c * CHUNK, CHUNK)] = total
        return 0

    lax.fori_loop(0, chunks, add_up, 0)
    gradient_copy = pltpu.make_async_copy(gradient, gradient_out, load_sem.at[2])
    gradient_copy.start()
    for j in others:
        back_copy(j).wait_send()
    field_copy.wait()
    adjoint_copy.wait()
    gradient_copy.wait()


def per_device(
    squared_courant,
    window_offset,
    field_last,
    field_after,
    adjoint_last,
    adjoint_after,
    source_place,
    source_wavelet,
    receiver_place,
    receiver_trace,
):
    _, depth, width, across = field_last.shape
    x = np.arange(width)
    taper = (np.sin(math.pi * (x + 0.5) / width) ** 2 / SCALE).astype(np.float32)
    taper = jnp.asarray(np.broadcast_to(taper[:, None], (width, across)))
    smem = pl.BlockSpec(memory_space=pltpu.SMEM)
    vmem = pl.BlockSpec(memory_space=pltpu.VMEM)
    hbm = pl.BlockSpec(memory_space=pl.ANY)
    f32 = jnp.float32
    dma = pltpu.SemaphoreType.DMA
    field, adjoint, gradient = pl.pallas_call(
        kernel,
        out_shape=(
            jax.ShapeDtypeStruct((depth, width, across), f32),
            jax.ShapeDtypeStruct((depth, width, across), f32),
            jax.ShapeDtypeStruct((depth, WB, across), f32),
        ),
        in_specs=[smem] * 3 + [vmem] * 3 + [hbm] * 5,
        out_specs=(hbm, hbm, hbm),
        scratch_shapes=[
            pltpu.VMEM((2, 2, depth + 2 * HALO, width, across), f32),
            pltpu.VMEM((SPAN, depth, WB, across), f32),
            pltpu.VMEM((2, depth, width, across), f32),
            pltpu.VMEM((depth, width, across), f32),
            pltpu.VMEM((depth, width, across), f32),
            pltpu.VMEM((SPAN + 4, depth, WB, across), f32),
            pltpu.VMEM((SPAN, depth, WB, across), f32),
            pltpu.VMEM((SPAN, depth, WB, across), f32),
            pltpu.VMEM((depth, WB, across), f32),
            pltpu.VMEM((depth * width, across), jnp.bfloat16),
            pltpu.VMEM((STEPS, across, 2 * across), jnp.bfloat16),
            dma((5,)),
            dma((STEPS, 2, 2)),
            dma((STEPS, 2, 2)),
            dma((SPAN,)),
            dma((SPAN,)),
            dma((SPAN,)),
            dma((SPAN,)),
        ],
        compiler_params=pltpu.CompilerParams(
            collective_id=0, has_side_effects=True, vmem_limit_bytes=40 * 1024 * 1024
        ),
        name="inversion",
    )(
        window_offset,
        source_place[0],
        source_wavelet[0],
        receiver_place[0],
        receiver_trace[0],
        taper,
        squared_courant,
        field_last[0],
        field_after[0],
        adjoint_last[0],
        adjoint_after[0],
    )
    return field[None], adjoint[None], gradient


def solution(mesh):
    placed = (
        P("gz", "shot", None),
        P("shot"),
        P("shot", "gz", None, None),
        P("shot", "gz", None, None),
        P("shot", "gz", None, None),
        P("shot", "gz", None, None),
        P("shot", None),
        P("shot", None),
        P("shot", None, None),
        P("shot", None, None),
    )
    return jax.shard_map(
        per_device,
        mesh=mesh,
        in_specs=placed,
        out_specs=(P("shot", "gz", None, None), P("shot", "gz", None, None), P("gz", "shot", None)),
        check_vma=False,
    )
```

profile of v0, /device:TPU:1, one launch (start us, length us, event | category | flops | bytes accessed | tf_op | source)
XLA Modules:
  0.0 138.5 jit_solution(17445907644247733681)
XLA Ops:
  1.3 0.0 copy-start.8
  1.3 0.7 copy-done.8
  2.0 0.0 copy-start.9
  2.0 0.7 copy-done.9
  2.6 0.0 copy-start.5
  2.6 0.0 copy-start.6
  2.6 0.0 copy-start.7
  2.6 0.1 jit_solution_.3.taper_ref
  2.7 0.6 copy-done.5
  3.3 0.0 copy-done.6
  3.3 0.0 copy-done.7
  3.3 0.0 copy-start
  3.3 1.2 copy-done
  4.5 0.0 copy-start.1
  4.5 1.2 copy-done.1
  5.8 1.2 copy-done.2
  7.0 0.0 copy-start.3
  7.0 1.2 copy-done.3
  8.2 0.0 copy-start.4
  8.2 0.9 copy-done.4
  9.1 126.8 %inversion.1 = (f32[32,64,128]{2,1,0:T(8,128)S(1)}, f32[32,64,128]{2,1,0:T(8,128)S(1)}, f32[32,8,128]{2,1,0:T(8,128)S(1)}) custom-call(s32[1]{0:T(128)S(6)} %copy.20.offset_ref, s32[3]{0:T(128)S(1)} %bitcast.20, f32[4]{0:T(128)S(1)} %bitcast.21, s32[3,128]{1,0:T(4,128)S(1)} %bitcast.18, f32[4,128]{1,0:T(4,128)S(1)} %bitcast.19, ...), custom_call_target="tpu_custom_call" | custom-call | tf_op jit(solution)/shard_map/inversion/pallas_call | solution.py:374
  135.9 1.0 copy.21
  136.9 1.0 copy.22
  137.9 0.7 copy.23
  (2 shorter events, 0.0 us)
Async XLA Ops:
  1.3 0.7 copy-start.8
  2.0 0.7 copy-start.9
  2.6 0.7 copy-start.5
  2.6 0.7 copy-start.6
  2.6 0.7 copy-start.7
  3.3 1.2 copy-start
  4.5 1.2 copy-start.1
  5.8 1.2 copy-start.2
  7.0 1.2 copy-start.3
  8.2 0.9 copy-start.4
where the time goes:
time: 141 us; the launch traced here: 139 us
  Pallas kernels  127 us (90%)
  local copies, waits for them, and re-layouts  10.4 us (7%)
    pallas_call x1, Pallas kernels, per_device(): pl.pallas_call(kernel, out_shape=(jax.ShapeDtypeStruct((depth, width, acr...  127 us
    unnamed x24, local copies, waits for them, and re-layouts  10.3 us

commit v1 on v0

--- a/solution.py
+++ b/solution.py
@@ -10,6 +10,8 @@
 from jax.sharding import PartitionSpec as P
 
 WB = 8
+COLS = 4
+FIRST = (0, 1, -2, -1)
 SPREAD = 2
 STEPS = 4
 SPAN = WB + 2 * SPREAD
@@ -41,9 +43,9 @@
     offset_ref,
     spot_ref,
     wavelet_ref,
-    receivers_ref,
-    traces_ref,
-    taper_ref,
+    receivers_in,
+    traces_in,
+    taper_in,
     courant_ref,
     field_last,
     field_after,
@@ -59,17 +61,26 @@
     imaging,
     shown,
     outgoing,
-    arriving,
+    from_row,
+    sums,
+    from_rows,
     gradient,
+    receivers_ref,
+    traces_ref,
+    taper_ref,
     hits,
     amounts,
     load_sem,
     halo_send,
     halo_recv,
+    row_send,
+    row_recv,
     piece_send,
     piece_recv,
     back_send,
     back_recv,
+    sum_send,
+    sum_recv,
 ):
     shot = lax.axis_index("shot")
     slab = lax.axis_index("gz")
@@ -80,15 +91,34 @@
     has = (slab > 0, slab < slabs - 1)
     beside = (jnp.maximum(slab - 1, 0), jnp.minimum(slab + 1, slabs - 1))
 
-    def partner(k):
-        return lax.rem(shot + k + shots, shots)
+    row, col = shot // COLS, lax.rem(shot, COLS)
+    rows = shots // COLS
+    has_extra = col != 1
+    extra_row = jnp.where(col == 0, 3, -1)
+
+    def in_row(dx):
+        return row * COLS + lax.rem(col + dx, COLS)
+
+    def in_column(r):
+        return lax.rem(row + r + rows, rows) * COLS + col
+
+    def first_row(source, dx):
+        return (source + FIRST[dx] - lax.rem(source + dx, COLS)) // COLS
 
     loads = []
     for i, (buffer, which, source) in enumerate(
         ((0, 0, field_last), (0, 1, adjoint_last), (1, 0, field_after), (1, 1, adjoint_after))
     ):
         loads.append(pltpu.make_async_copy(source, fields.at[buffer, which, pl.ds(HALO, depth)], load_sem.at[i]))
-    loads.append(pltpu.make_async_copy(courant_ref, pieces.at[SPREAD], load_sem.at[4]))
+    for i, (source, place) in enumerate(
+        (
+            (courant_ref, pieces.at[SPREAD]),
+            (receivers_in, receivers_ref),
+            (traces_in, traces_ref),
+            (taper_in, taper_ref),
+        )
+    ):
+        loads.append(pltpu.make_async_copy(source, place, load_sem.at[4 + i]))
     for copy in loads:
         copy.start()
 
@@ -102,9 +132,10 @@
                     fields[buffer, which, pl.ds(place, HALO)] = blank
 
     barrier = pltpu.get_barrier_semaphore()
-    for k in range(-(SPAN - SPREAD - 1), SPAN - SPREAD):
-        if k != 0:
-            pl.semaphore_signal(barrier, inc=1, device_id={"shot": partner(k)}, device_id_type=MESH)
+    for dx in range(1, COLS):
+        pl.semaphore_signal(barrier, inc=1, device_id={"shot": in_row(dx)}, device_id_type=MESH)
+    for r in (-3, -2, -1, 1, 2, 3):
+        pl.semaphore_signal(barrier, inc=1, device_id={"shot": in_column(r)}, device_id_type=MESH)
     for side in range(2):
 
         @pl.when(has[side])
@@ -112,7 +143,7 @@
             pl.semaphore_signal(barrier, inc=1, device_id={"gz": beside[side]}, device_id_type=MESH)
 
     beside_count = jnp.where(has[0], 1, 0) + jnp.where(has[1], 1, 0)
-    pl.semaphore_wait(barrier, 2 * (SPAN - SPREAD - 1) + beside_count)
+    pl.semaphore_wait(barrier, COLS - 1 + 6 + beside_count)
 
     def halo(turn, which, side):
         place = HALO if side == 0 else depth
@@ -145,46 +176,128 @@
         def _():
             halo(turn, which, side).wait_send()
 
-    def piece_copy(j):
+    def row_copy(i):
         return pltpu.make_async_remote_copy(
             src_ref=courant_ref,
-            dst_ref=pieces.at[j],
-            send_sem=piece_send.at[j],
-            recv_sem=piece_recv.at[j],
-            device_id={"shot": partner(SPREAD - j)},
+            dst_ref=pieces.at[(SPREAD + COLS, SPREAD + 2 * COLS, SPAN)[i]],
+            send_sem=row_send.at[i],
+            recv_sem=row_recv.at[i],
+            device_id={"shot": in_column((-1, -2, -extra_row)[i])},
             device_id_type=MESH,
         )
 
-    def back_copy(j):
+    def piece_copy(dx, r):
+        target = lax.rem(col + dx, COLS)
+        slot = COLS * r + col - target + SPREAD
+        held = jnp.where((r >= 0) & (r <= 2), SPREAD + COLS * r, SPAN)
         return pltpu.make_async_remote_copy(
-            src_ref=outgoing.at[j],
-            dst_ref=arriving.at[j],
-            send_sem=back_send.at[j],
-            recv_sem=back_recv.at[j],
-            device_id={"shot": partner(j - SPREAD)},
+            src_ref=pieces.at[held],
+            dst_ref=pieces.at[slot],
+            send_sem=piece_send.at[dx - 1, r - slab_row(dx)],
+            recv_sem=piece_recv.at[slot],
+            device_id={"shot": in_row(dx)},
             device_id_type=MESH,
         )
+
+    def slab_row(dx):
+        return first_row(lax.rem(col + dx, COLS), COLS - dx)
+
+    def piece_arrived(j):
+        pltpu.make_async_copy(pieces.at[j], pieces.at[j], piece_recv.at[j]).wait()
+
+    def part_copy(dx, r):
+        target = lax.rem(col + dx, COLS)
+        return pltpu.make_async_remote_copy(
+            src_ref=outgoing.at[COLS * r + target - col + SPREAD],
+            dst_ref=from_row.at[dx - 1, r - first_row(col, dx)],
+            send_sem=back_send.at[dx - 1, r - first_row(col, dx)],
+            recv_sem=back_recv.at[dx - 1, r - first_row(col, dx)],
+            device_id={"shot": in_row(dx)},
+            device_id_type=MESH,
+        )
+
+    def part_start(dx, r):
+        first = first_row(col, dx)
+
+        @pl.when((r >= first) & (r <= first + 2))
+        def _():
+            part_copy(dx, r).start()
+
+    def source_row(dx):
+        return first_row(lax.rem(col - dx + COLS, COLS), dx)
+
+    def part_arrived(dx, r):
+        first = source_row(dx)
+
+        @pl.when((r >= first) & (r <= first + 2))
+        def _():
+            place = from_row.at[dx - 1, r - first]
+            pltpu.make_async_copy(place, place, back_recv.at[dx - 1, r - first]).wait()
+
+    def summed(r, own, c):
+        place = pl.ds(pl.multiple_of(c * CHUNK, CHUNK), CHUNK)
+        total = outgoing[SPREAD + COLS * r, place] if own else jnp.zeros((CHUNK, WB, across), jnp.float32)
+        for dx in range(1, COLS):
+            at = r - source_row(dx)
+            total = total + from_row[dx - 1, jnp.where((at >= 0) & (at <= 2), at, 3), place]
+        return total
+
+    def sum_copy(i):
+        return pltpu.make_async_remote_copy(
+            src_ref=sums.at[i],
+            dst_ref=from_rows.at[i],
+            send_sem=sum_send.at[i],
+            recv_sem=sum_recv.at[i],
+            device_id={"shot": in_column((1, 2, extra_row)[i])},
+            device_id_type=MESH,
+        )
+
+    def sum_start(i):
+        r = (1, 2, extra_row)[i]
+        for dx in range(1, COLS):
+            part_arrived(dx, r)
+
+        def turn(c, _):
+            sums[i, pl.ds(pl.multiple_of(c * CHUNK, CHUNK), CHUNK)] = summed(r, i < 2, c)
+            return 0
+
+        lax.fori_loop(0, chunks, turn, 0)
+        sum_copy(i).start()
 
     for which in range(2):
         for side in range(2):
             halo_start(0, which, side)
-    others = [j for j in range(SPAN) if j != SPREAD]
-    for j in others:
-        piece_copy(j).start()
+    row_copy(0).start()
+
+    @pl.when(has_extra)
+    def _():
+        row_copy(2).start()
+
+    row_copy(1).start()
+    own_slab = loads.pop(4)
+    own_slab.wait()
+    for dx in range(1, COLS):
+
+        @pl.when(slab_row(dx) <= 0)
+        def _():
+            piece_copy(dx, 0).start()
+
 
     offset = offset_ref[0]
+    for copy in loads[4:]:
+        copy.wait()
     by_y = banded(2 * across, across, across)
     by_x = banded(width, 2 * width, width)
-    row = lax.broadcasted_iota(jnp.int32, (width * CHUNK, across), 0)
-    place = (receivers_ref[0:1, :] - slab * depth) * width + receivers_ref[1:2, :]
+    cell = lax.broadcasted_iota(jnp.int32, (width * CHUNK, across), 0)
+    place = (receivers_ref[0] - slab * depth) * width + receivers_ref[1]
 
     def mark(c, _):
         start = pl.multiple_of(c * CHUNK * width, CHUNK * width)
-        hits[pl.ds(start, CHUNK * width), :] = jnp.where(row + start == place, 1.0, 0.0).astype(jnp.bfloat16)
+        hits[pl.ds(start, CHUNK * width), :] = jnp.where(cell + start == place, 1.0, 0.0).astype(jnp.bfloat16)
         return 0
 
     lax.fori_loop(0, chunks, mark, 0)
-    along = lax.broadcasted_iota(jnp.int32, (across, across), 0) == receivers_ref[2:3, :]
+    along = lax.broadcasted_iota(jnp.int32, (across, across), 0) == receivers_ref[2]
     for step in range(STEPS):
         high, low = in_two(jnp.where(along, traces_ref[step : step + 1, :], 0.0))
         amounts[step, :, 0:across] = high
@@ -283,19 +396,46 @@
 
         lax.fori_loop(1, chunks - 1, turn, 0)
 
+    def pass_on_near():
+        row_copy(0).wait_recv()
+        for dx in (1, 3, 2):
+            piece_copy(dx, 1).start()
+
+        @pl.when(has_extra)
+        def _():
+            row_copy(2).wait_recv()
+
+        for dx in range(1, COLS):
+            first = slab_row(dx)
+
+            @pl.when(first != 0)
+            def _():
+                piece_copy(dx, jnp.where(first < 0, -1, 3)).start()
+
+    def pass_on_later():
+        row_copy(1).wait_recv()
+        for dx in range(1, COLS):
+
+            @pl.when(slab_row(dx) >= 0)
+            def _():
+                piece_copy(dx, 2).start()
+
     ends = (0, depth - CHUNK)
     for copy in loads[:2]:
         copy.wait()
-    for which in range(2):
-        inner(functools.partial(first_part, which))
+    inner(functools.partial(first_part, 0))
+    pass_on_near()
+    inner(functools.partial(first_part, 1))
     for which in range(2):
         for side in range(2):
             halo_arrived(0, which, side)
             first_part(which, ends[side])
-    for copy in loads[2:]:
+    for copy in loads[2:4]:
         copy.wait()
-    for j in others:
-        piece_copy(j).wait_recv()
+    pass_on_later()
+    for j in range(SPAN):
+        if j % COLS != SPREAD:
+            piece_arrived(j)
     for s in range(WB):
         model[:, s * WB : (s + 1) * WB, :] = pieces[offset + SPREAD + s] * (1.0 / SCALE)
     for which in range(2):
@@ -320,31 +460,57 @@
                 field_copy.start()
                 for j in range(SPAN):
                     outgoing[j] = shown[j + 2 - offset]
-                    if j != SPREAD:
-                        back_copy(j).start()
+                for r in (2, -1, 3, 1, 0):
+                    for dx in (1, 3, 2):
+                        part_start(dx, r)
+                from_row[:, 3] = jnp.zeros((COLS - 1, depth, WB, across), jnp.float32)
     adjoint_copy = pltpu.make_async_copy(fields.at[0, 1, pl.ds(HALO, depth)], adjoint_out, load_sem.at[1])
     adjoint_copy.start()
+    sum_start(1)
+
+    @pl.when(has_extra)
+    def _():
+        sum_start(2)
+
+    sum_start(0)
+    for dx in range(1, COLS):
+        part_arrived(dx, 0)
+    for i in (0, 1):
+        sum_copy(i).wait_recv()
+
+    @pl.when(has_extra)
+    def _():
+        sum_copy(2).wait_recv()
+
+    @pl.when(jnp.logical_not(has_extra))
+    def _():
+        from_rows[2] = jnp.zeros((depth, WB, across), jnp.float32)
+
+    def add_up(c, _):
+        place = pl.ds(pl.multiple_of(c * CHUNK, CHUNK), CHUNK)
+        gradient[place] = summed(0, True, c) + from_rows[0, place] + from_rows[1, place] + from_rows[2, place]
+        return 0
+
+    lax.fori_loop(0, chunks, add_up, 0)
+    gradient_copy = pltpu.make_async_copy(gradient, gradient_out, load_sem.at[2])
+    gradient_copy.start()
     for which in range(2):
         for side in range(2):
             halo_sent(0, which, side)
             halo_sent(STEPS - 1, which, side)
-    for j in others:
-        piece_copy(j).wait_send()
-    for j in others:
-        back_copy(j).wait_recv()
-
-    def add_up(c, _):
-        total = outgoing[SPREAD, pl.ds(c * CHUNK, CHUNK)]
-        for j in others:
-            total = total + arriving[j, pl.ds(c * CHUNK, CHUNK)]
-        gradient[pl.ds(c * CHUNK, CHUNK)] = total
-        return 0
-
-    lax.fori_loop(0, chunks, add_up, 0)
-    gradient_copy = pltpu.make_async_copy(gradient, gradient_out, load_sem.at[2])
-    gradient_copy.start()
-    for j in others:
-        back_copy(j).wait_send()
+    for i in (0, 1):
+        row_copy(i).wait_send()
+        sum_copy(i).wait_send()
+
+    @pl.when(has_extra)
+    def _():
+        row_copy(2).wait_send()
+        sum_copy(2).wait_send()
+
+    for dx in range(1, COLS):
+        for t in range(3):
+            piece_copy(dx, slab_row(dx) + t).wait_send()
+            part_copy(dx, first_row(col, dx) + t).wait_send()
     field_copy.wait()
     adjoint_copy.wait()
     gradient_copy.wait()
@@ -367,7 +533,6 @@
     taper = (np.sin(math.pi * (x + 0.5) / width) ** 2 / SCALE).astype(np.float32)
     taper = jnp.asarray(np.broadcast_to(taper[:, None], (width, across)))
     smem = pl.BlockSpec(memory_space=pltpu.SMEM)
-    vmem = pl.BlockSpec(memory_space=pltpu.VMEM)
     hbm = pl.BlockSpec(memory_space=pl.ANY)
     f32 = jnp.float32
     dma = pltpu.SemaphoreType.DMA
@@ -378,37 +543,46 @@
             jax.ShapeDtypeStruct((depth, width, across), f32),
             jax.ShapeDtypeStruct((depth, WB, across), f32),
         ),
-        in_specs=[smem] * 3 + [vmem] * 3 + [hbm] * 5,
+        in_specs=[smem] * 3 + [hbm] * 8,
         out_specs=(hbm, hbm, hbm),
         scratch_shapes=[
             pltpu.VMEM((2, 2, depth + 2 * HALO, width, across), f32),
-            pltpu.VMEM((SPAN, depth, WB, across), f32),
+            pltpu.VMEM((SPAN + 1, depth, WB, across), f32),
             pltpu.VMEM((2, depth, width, across), f32),
             pltpu.VMEM((depth, width, across), f32),
             pltpu.VMEM((depth, width, across), f32),
             pltpu.VMEM((SPAN + 4, depth, WB, across), f32),
             pltpu.VMEM((SPAN, depth, WB, across), f32),
-            pltpu.VMEM((SPAN, depth, WB, across), f32),
+            pltpu.VMEM((COLS - 1, 4, depth, WB, across), f32),
+            pltpu.VMEM((3, depth, WB, across), f32),
+            pltpu.VMEM((3, depth, WB, across), f32),
             pltpu.VMEM((depth, WB, across), f32),
+            pltpu.VMEM((3, 1, across), jnp.int32),
+            pltpu.VMEM((STEPS, across), f32),
+            pltpu.VMEM((width, across), f32),
             pltpu.VMEM((depth * width, across), jnp.bfloat16),
             pltpu.VMEM((STEPS, across, 2 * across), jnp.bfloat16),
-            dma((5,)),
+            dma((8,)),
             dma((STEPS, 2, 2)),
             dma((STEPS, 2, 2)),
+            dma((3,)),
+            dma((3,)),
+            dma((COLS - 1, 3)),
             dma((SPAN,)),
-            dma((SPAN,)),
-            dma((SPAN,)),
-            dma((SPAN,)),
+            dma((COLS - 1, 3)),
+            dma((COLS - 1, 3)),
+            dma((3,)),
+            dma((3,)),
         ],
         compiler_params=pltpu.CompilerParams(
-            collective_id=0, has_side_effects=True, vmem_limit_bytes=40 * 1024 * 1024
+            collective_id=0, has_side_effects=True, vmem_limit_bytes=56 * 1024 * 1024
         ),
         name="inversion",
     )(
         window_offset,
         source_place[0],
         source_wavelet[0],
-        receiver_place[0],
+        receiver_place.transpose(1, 0, 2),
         receiver_trace[0],
         taper,
         squared_courant,

time: 141 us -> 83.4 us (0.59); the launches traced: 139 us -> 83.3 us
  Pallas kernels: 127 us -> 76.5 us
  local copies, waits for them, and re-layouts: 10.4 us -> 5.42 us
    pallas_call x1, Pallas kernels: 127 us -> 76.5 us  [per_device(): pl.pallas_call(kernel, out_shape=(jax.ShapeDtypeStruct((depth, width, acr...]
    unnamed x24 -> x9, local copies, waits for them, and re-layouts: 10.3 us -> 4.73 us
where the time goes in v1:
time: 83.4 us; the launch traced here: 83.3 us
  Pallas kernels  76.5 us (92%)
  local copies, waits for them, and re-layouts  5.42 us (6%)
  between operations  1.3 us (2%)
    pallas_call x1, Pallas kernels, per_device(): pl.pallas_call(kernel, out_shape=(jax.ShapeDtypeStruct((depth, width, acr...  76.5 us
    unnamed x9, local copies, waits for them, and re-layouts  4.73 us

profile of v1, /device:TPU:1, one launch (start us, length us, event | category | flops | bytes accessed | tf_op | source)
XLA Modules:
  0.0 83.3 jit_solution(3346090272895408422)
XLA Ops:
  1.3 0.0 copy-start.2
  1.3 0.6 copy-done.2
  1.9 0.7 jit_solution_.3.taper_in
  2.6 76.5 %inversion.1 = (f32[32,64,128]{2,1,0:T(8,128)}, f32[32,64,128]{2,1,0:T(8,128)}, f32[32,8,128]{2,1,0:T(8,128)}) custom-call(s32[1]{0:T(128)S(6)} %copy.17.offset_ref, s32[3]{0:T(128)} %bitcast.18, f32[4]{0:T(128)} %bitcast.19, s32[3,1,128]{2,1,0:T(1,128)} %bitcast.17, f32[4,128]{1,0:T(4,128)} %bitcast.16, f32[64,128]{1,0:T(8,128)} %jit_solution_.3.taper_in, ...), custom_call_target="tpu_custom_call" | custom-call | tf_op jit(solution)/shard_map/inversion/pallas_call | solution.py:539
  79.2 0.0 copy-start
  79.2 2.4 %copy.18 = f32[1,32,64,128]{3,2,1,0:T(8,128)} copy(f32[1,32,64,128]{3,2,1,0:T(8,128)} %bitcast.11) | data formatting | bytes 2097152
  81.6 0.0 copy-done
  81.6 0.0 copy-start.1
  81.6 1.0 %copy.19 = f32[1,32,64,128]{3,2,1,0:T(8,128)} copy(f32[1,32,64,128]{3,2,1,0:T(8,128)S(1)} %bitcast.10) | data formatting | bytes 2097152
  82.6 0.1 copy-done.1
  82.6 0.7 copy.20
Async XLA Ops:
  1.3 0.7 copy-start.2
  79.2 2.4 %copy-start = (f32[32,64,128]{2,1,0:T(8,128)S(1)}, f32[32,64,128]{2,1,0:T(8,128)}, u32[]{:S(2)}) copy-start(f32[32,64,128]{2,1,0:T(8,128)} %get-tuple-element.7) | copy-start | bytes 3145732
  81.6 1.0 %copy-start.1 = (f32[32,8,128]{2,1,0:T(8,128)S(1)}, f32[32,8,128]{2,1,0:T(8,128)}, u32[]{:S(2)}) copy-start(f32[32,8,128]{2,1,0:T(8,128)} %get-tuple-element.14) | copy-start | bytes 393220

commit v2 on v1

--- a/solution.py
+++ b/solution.py
@@ -3,7 +3,6 @@
 
 import jax
 import jax.numpy as jnp
-import numpy as np
 from jax import lax
 from jax.experimental import pallas as pl
 from jax.experimental.pallas import tpu as pltpu
@@ -17,6 +16,7 @@
 SPAN = WB + 2 * SPREAD
 HALO = 4
 CHUNK = 4
+BLOCK = 12
 SCALE = 5040.0
 CENTRE = -3.0 * 14350.0
 SIDE = (8064.0, -1008.0, 128.0, -9.0)
@@ -45,7 +45,6 @@
     wavelet_ref,
     receivers_in,
     traces_in,
-    taper_in,
     courant_ref,
     field_last,
     field_after,
@@ -54,7 +53,10 @@
     field_out,
     adjoint_out,
     gradient_out,
-    fields,
+    field_a,
+    adjoint_a,
+    field_b,
+    adjoint_b,
     pieces,
     laps,
     model,
@@ -64,7 +66,6 @@
     from_row,
     sums,
     from_rows,
-    gradient,
     receivers_ref,
     traces_ref,
     taper_ref,
@@ -82,6 +83,7 @@
     sum_send,
     sum_recv,
 ):
+    fields = ((field_a, adjoint_a), (field_b, adjoint_b))
     shot = lax.axis_index("shot")
     slab = lax.axis_index("gz")
     shots = lax.axis_size("shot")
@@ -109,13 +111,12 @@
     for i, (buffer, which, source) in enumerate(
         ((0, 0, field_last), (0, 1, adjoint_last), (1, 0, field_after), (1, 1, adjoint_after))
     ):
-        loads.append(pltpu.make_async_copy(source, fields.at[buffer, which, pl.ds(HALO, depth)], load_sem.at[i]))
+        loads.append(pltpu.make_async_copy(source, fields[buffer][which].at[pl.ds(HALO, depth)], load_sem.at[i]))
     for i, (source, place) in enumerate(
         (
             (courant_ref, pieces.at[SPREAD]),
             (receivers_in, receivers_ref),
             (traces_in, traces_ref),
-            (taper_in, taper_ref),
         )
     ):
         loads.append(pltpu.make_async_copy(source, place, load_sem.at[4 + i]))
@@ -129,7 +130,7 @@
         def _():
             for buffer in range(2):
                 for which in range(2):
-                    fields[buffer, which, pl.ds(place, HALO)] = blank
+                    fields[buffer][which][pl.ds(place, HALO)] = blank
 
     barrier = pltpu.get_barrier_semaphore()
     for dx in range(1, COLS):
@@ -151,10 +152,10 @@
         if turn == 0:
             source = (field_last, adjoint_last)[which].at[pl.ds(place - HALO, HALO)]
         else:
-            source = fields.at[turn % 2, which, pl.ds(place, HALO)]
+            source = fields[turn % 2][which].at[pl.ds(place, HALO)]
         return pltpu.make_async_remote_copy(
             src_ref=source,
-            dst_ref=fields.at[turn % 2, which, pl.ds(landing, HALO)],
+            dst_ref=fields[turn % 2][which].at[pl.ds(landing, HALO)],
             send_sem=halo_send.at[turn, which, side],
             recv_sem=halo_recv.at[turn, which, side],
             device_id={"gz": beside[side]},
@@ -302,6 +303,8 @@
         high, low = in_two(jnp.where(along, traces_ref[step : step + 1, :], 0.0))
         amounts[step, :, 0:across] = high
         amounts[step, :, across : 2 * across] = low
+    across_x = lax.broadcasted_iota(jnp.int32, (width, across), 0).astype(jnp.float32)
+    taper_ref[...] = jnp.sin((across_x + 0.5) * (math.pi / width)) ** 2 * (1.0 / SCALE)
     spot = jnp.where(
         (lax.broadcasted_iota(jnp.int32, (width, across), 0) == spot_ref[1])
         & (lax.broadcasted_iota(jnp.int32, (width, across), 1) == spot_ref[2]),
@@ -312,33 +315,24 @@
     shown[pl.ds(0, 4)] = jnp.zeros((4, depth, WB, across), jnp.float32)
     shown[pl.ds(12, 4)] = jnp.zeros((4, depth, WB, across), jnp.float32)
 
-    def stencil(buffer, which, z0):
-        centre = fields[buffer, which, pl.ds(z0 + HALO, CHUNK)]
-        high, low = in_two(centre)
-        rows = CHUNK * width
+    def flat(high, low, planes):
+        rows = planes * width
         left = jnp.concatenate([high.reshape(rows, across), low.reshape(rows, across)], axis=1)
         in_y = jnp.dot(left, by_y, preferred_element_type=jnp.float32)
         right = jnp.concatenate(
-            [
-                jnp.concatenate([high[c] for c in range(CHUNK)], axis=1),
-                jnp.concatenate([low[c] for c in range(CHUNK)], axis=1),
-            ],
-            axis=0,
+            [jnp.concatenate([part[c] for c in range(planes)], axis=1) for part in (high, low)], axis=0
         )
         in_x = jnp.dot(by_x, right, preferred_element_type=jnp.float32)
-        result = []
-        for c in range(CHUNK):
-            total = CENTRE * centre[c] + in_y[c * width : (c + 1) * width] + in_x[:, c * across : (c + 1) * across]
-            for k in range(1, 5):
-                above = fields[buffer, which, z0 + HALO + c + k]
-                below = fields[buffer, which, z0 + HALO + c - k]
-                total = total + SIDE[k - 1] * (above + below)
-            result.append(total)
-        return centre, result
-
-    def injected(step, z0):
-        start = pl.multiple_of(z0 * width, CHUNK * width)
-        found = hits[pl.ds(start, CHUNK * width), :]
+        return in_y, in_x
+
+    def spans(starts, planes):
+        return [(z0, i * planes) for i, z0 in enumerate(starts)]
+
+    def injected(step, starts, planes):
+        found = []
+        for z0 in starts:
+            found.append(hits[pl.ds(pl.multiple_of(z0 * width, CHUNK * width), planes * width), :])
+        found = jnp.concatenate(found, axis=0)
         return lax.dot_general(
             jnp.concatenate([found, found], axis=1),
             amounts[step],
@@ -346,55 +340,81 @@
             preferred_element_type=jnp.float32,
         )
 
-    def advance(step, which, z0, centre, lap):
-        later = 1 - step % 2
-        if which == 1:
-            added = injected(step, z0)
-        for c in range(CHUNK):
+    def laplace(now, starts, planes, use):
+        high, low = in_two(jnp.concatenate([now[pl.ds(z0 + HALO, planes)] for z0 in starts], axis=0))
+        in_y, in_x = flat(high, low, planes * len(starts))
+        for s in range(width // WB):
+            tile = pl.ds(s * WB, WB)
+            for z0, first in spans(starts, planes):
+                line = [now[z0 + c, tile] for c in range(planes + 2 * HALO)]
+                for c in range(planes):
+                    at = first + c
+                    centre = line[c + HALO]
+                    total = CENTRE * centre + in_y[at * width + s * WB : at * width + (s + 1) * WB]
+                    total = total + in_x[s * WB : (s + 1) * WB, at * across : (at + 1) * across]
+                    for k in range(1, 5):
+                        total = total + SIDE[k - 1] * (line[c + HALO + k] + line[c + HALO - k])
+                    use(z0 + c, at, s, tile, centre, total)
+
+    def see(step, z, s, tile, lap):
+        seen = fields[step % 2][1][z + HALO, tile] * lap
+        if step > 0:
+            seen = imaging[z, tile] + seen
+        if step < STEPS - 1:
+            imaging[z, tile] = seen
+        else:
+            shown[4 + s, z] = taper_ref[tile] * seen
+
+    def advance(step, which, z, tile, centre, lap, extra):
+        later = fields[1 - step % 2][which]
+        new = 2.0 * centre - later[z + HALO, tile] + model[z, tile] * lap + extra
+        if step < STEPS - 1:
+            later[z + HALO, tile] = new
+        else:
+            (field_out, adjoint_out)[which][z, tile] = new
+
+    def extras(step, which, starts, planes):
+        if which == 0:
+            return lambda z, at, s, tile: spot[s * WB : (s + 1) * WB] * jnp.where(
+                z == spot_depth, wavelet_ref[step], 0.0
+            )
+        added = injected(step, starts, planes)
+        return lambda z, at, s, tile: added[at * width + s * WB : at * width + (s + 1) * WB]
+
+    def first_part(which, starts, planes):
+        def use(z, at, s, tile, centre, lap):
+            laps[which, z, tile] = lap
             if which == 0:
-                extra = spot * jnp.where(z0 + c == spot_depth, wavelet_ref[step], 0.0)
-            else:
-                extra = added[c * width : (c + 1) * width]
-            fields[later, which, z0 + HALO + c] = (
-                2.0 * centre[c] - fields[later, which, z0 + HALO + c] + model[z0 + c] * lap[c] + extra
-            )
-
-    def see(step, z0, lap):
-        now = step % 2
-        for c in range(CHUNK):
-            seen = fields[now, 1, z0 + HALO + c] * lap[c]
-            if step > 0:
-                seen = imaging[z0 + c] + seen
-            if step < STEPS - 1:
-                imaging[z0 + c] = seen
-            else:
-                weighted = taper_ref[...] * seen
-                for s in range(WB):
-                    shown[4 + s, z0 + c] = weighted[s * WB : (s + 1) * WB]
-
-    def first_part(which, z0):
-        _, lap = stencil(0, which, z0)
-        for c in range(CHUNK):
-            laps[which, z0 + c] = lap[c]
-        if which == 0:
-            see(0, z0, lap)
-
-    def second_part(which, z0):
-        centre = fields[0, which, pl.ds(z0 + HALO, CHUNK)]
-        advance(0, which, z0, centre, [laps[which, z0 + c] for c in range(CHUNK)])
-
-    def whole(step, which, z0):
-        centre, lap = stencil(step % 2, which, z0)
-        if which == 0:
-            see(step, z0, lap)
-        advance(step, which, z0, centre, lap)
+                see(0, z, s, tile, lap)
+
+        laplace(fields[0][which], starts, planes, use)
+
+    def second_part(which, starts, planes):
+        extra = extras(0, which, starts, planes)
+        for s in range(width // WB):
+            tile = pl.ds(s * WB, WB)
+            for z0, first in spans(starts, planes):
+                for c in range(planes):
+                    z = z0 + c
+                    centre = fields[0][which][z + HALO, tile]
+                    advance(0, which, z, tile, centre, laps[which, z, tile], extra(z, first + c, s, tile))
+
+    def whole(step, which, starts, planes):
+        extra = extras(step, which, starts, planes)
+
+        def use(z, at, s, tile, centre, lap):
+            if which == 0:
+                see(step, z, s, tile, lap)
+            advance(step, which, z, tile, centre, lap, extra(z, at, s, tile))
+
+        laplace(fields[step % 2][which], starts, planes, use)
 
     def inner(body):
         def turn(c, _):
-            body(pl.multiple_of(c * CHUNK, CHUNK))
+            body([pl.multiple_of(c * BLOCK + HALO, CHUNK)], BLOCK)
             return 0
 
-        lax.fori_loop(1, chunks - 1, turn, 0)
+        lax.fori_loop(0, (depth - 2 * HALO) // BLOCK, turn, 0)
 
     def pass_on_near():
         row_copy(0).wait_recv()
@@ -429,7 +449,7 @@
     for which in range(2):
         for side in range(2):
             halo_arrived(0, which, side)
-            first_part(which, ends[side])
+        first_part(which, ends, CHUNK)
     for copy in loads[2:4]:
         copy.wait()
     pass_on_later()
@@ -439,8 +459,8 @@
     for s in range(WB):
         model[:, s * WB : (s + 1) * WB, :] = pieces[offset + SPREAD + s] * (1.0 / SCALE)
     for which in range(2):
+        second_part(which, ends, CHUNK)
         for side in range(2):
-            second_part(which, ends[side])
             halo_start(1, which, side)
     for which in range(2):
         inner(functools.partial(second_part, which))
@@ -451,21 +471,18 @@
                 halo_arrived(step, which, side)
                 if step > 1:
                     halo_sent(step - 1, which, side)
-                whole(step, which, ends[side])
-                if step < STEPS - 1:
+            whole(step, which, ends, CHUNK)
+            if step < STEPS - 1:
+                for side in range(2):
                     halo_start(step + 1, which, side)
             inner(functools.partial(whole, step, which))
             if step == STEPS - 1 and which == 0:
-                field_copy = pltpu.make_async_copy(fields.at[0, 0, pl.ds(HALO, depth)], field_out, load_sem.at[0])
-                field_copy.start()
                 for j in range(SPAN):
                     outgoing[j] = shown[j + 2 - offset]
                 for r in (2, -1, 3, 1, 0):
                     for dx in (1, 3, 2):
                         part_start(dx, r)
                 from_row[:, 3] = jnp.zeros((COLS - 1, depth, WB, across), jnp.float32)
-    adjoint_copy = pltpu.make_async_copy(fields.at[0, 1, pl.ds(HALO, depth)], adjoint_out, load_sem.at[1])
-    adjoint_copy.start()
     sum_start(1)
 
     @pl.when(has_extra)
@@ -488,12 +505,10 @@
 
     def add_up(c, _):
         place = pl.ds(pl.multiple_of(c * CHUNK, CHUNK), CHUNK)
-        gradient[place] = summed(0, True, c) + from_rows[0, place] + from_rows[1, place] + from_rows[2, place]
+        gradient_out[place] = summed(0, True, c) + from_rows[0, place] + from_rows[1, place] + from_rows[2, place]
         return 0
 
     lax.fori_loop(0, chunks, add_up, 0)
-    gradient_copy = pltpu.make_async_copy(gradient, gradient_out, load_sem.at[2])
-    gradient_copy.start()
     for which in range(2):
         for side in range(2):
             halo_sent(0, which, side)
@@ -511,9 +526,14 @@
         for t in range(3):
             piece_copy(dx, slab_row(dx) + t).wait_send()
             part_copy(dx, first_row(col, dx) + t).wait_send()
-    field_copy.wait()
-    adjoint_copy.wait()
-    gradient_copy.wait()
+
+
+def write_out(*refs):
+    copies = [pltpu.make_async_copy(refs[i], refs[3 + i], refs[6].at[i]) for i in range(3)]
+    for copy in copies:
+        copy.start()
+    for copy in copies:
+        copy.wait()
 
 
 def per_device(
@@ -529,24 +549,22 @@
     receiver_trace,
 ):
     _, depth, width, across = field_last.shape
-    x = np.arange(width)
-    taper = (np.sin(math.pi * (x + 0.5) / width) ** 2 / SCALE).astype(np.float32)
-    taper = jnp.asarray(np.broadcast_to(taper[:, None], (width, across)))
     smem = pl.BlockSpec(memory_space=pltpu.SMEM)
+    vmem = pl.BlockSpec(memory_space=pltpu.VMEM)
     hbm = pl.BlockSpec(memory_space=pl.ANY)
     f32 = jnp.float32
     dma = pltpu.SemaphoreType.DMA
     field, adjoint, gradient = pl.pallas_call(
         kernel,
         out_shape=(
-            jax.ShapeDtypeStruct((depth, width, across), f32),
-            jax.ShapeDtypeStruct((depth, width, across), f32),
-            jax.ShapeDtypeStruct((depth, WB, across), f32),
+            pltpu.VMEM((depth, width, across), f32),
+            pltpu.VMEM((depth, width, across), f32),
+            pltpu.VMEM((depth, WB, across), f32),
         ),
-        in_specs=[smem] * 3 + [hbm] * 8,
-        out_specs=(hbm, hbm, hbm),
+        in_specs=[smem] * 3 + [hbm] * 7,
+        out_specs=(vmem, vmem, vmem),
         scratch_shapes=[
-            pltpu.VMEM((2, 2, depth + 2 * HALO, width, across), f32),
+            *[pltpu.VMEM((depth + 2 * HALO, width, across), f32)] * 4,
             pltpu.VMEM((SPAN + 1, depth, WB, across), f32),
             pltpu.VMEM((2, depth, width, across), f32),
             pltpu.VMEM((depth, width, across), f32),
@@ -556,13 +574,12 @@
             pltpu.VMEM((COLS - 1, 4, depth, WB, across), f32),
             pltpu.VMEM((3, depth, WB, across), f32),
             pltpu.VMEM((3, depth, WB, across), f32),
-            pltpu.VMEM((depth, WB, across), f32),
             pltpu.VMEM((3, 1, across), jnp.int32),
             pltpu.VMEM((STEPS, across), f32),
             pltpu.VMEM((width, across), f32),
             pltpu.VMEM((depth * width, across), jnp.bfloat16),
             pltpu.VMEM((STEPS, across, 2 * across), jnp.bfloat16),
-            dma((8,)),
+            dma((7,)),
             dma((STEPS, 2, 2)),
             dma((STEPS, 2, 2)),
             dma((3,)),
@@ -584,14 +601,22 @@
         source_wavelet[0],
         receiver_place.transpose(1, 0, 2),
         receiver_trace[0],
-        taper,
         squared_courant,
         field_last[0],
         field_after[0],
         adjoint_last[0],
         adjoint_after[0],
     )
-    return field[None], adjoint[None], gradient
+    results = pl.pallas_call(
+        write_out,
+        out_shape=tuple(jax.ShapeDtypeStruct(x.shape, f32) for x in (field, adjoint, gradient)),
+        in_specs=[vmem] * 3,
+        out_specs=(hbm, hbm, hbm),
+        scratch_shapes=[dma((3,))],
+        compiler_params=pltpu.CompilerParams(vmem_limit_bytes=4 * 1024 * 1024),
+        name="write_out",
+    )(field, adjoint, gradient)
+    return results[0][None], results[1][None], results[2]
 
 
 def solution(mesh):

time: 83.4 us -> 77.8 us (0.933)
  local copies, waits for them, and re-layouts: 5.42 us -> 0 us
    unnamed x9 -> x0, local copies, waits for them, and re-layouts: 4.73 us -> none
    pallas_call x1 -> x2, Pallas kernels: 76.5 us -> 76.4 us  [the longest x1 75 us: per_device(): pl.pallas_call(kernel, out_shape=(pltpu.VMEM((depth, width, across), f32)...]
where the time goes in v2:
time: 77.8 us; the launch traced here: 77.7 us
  Pallas kernels  76.4 us (98%)
  between operations  1.29 us (2%)
    pallas_call x1, Pallas kernels, per_device(): pl.pallas_call(kernel, out_shape=(pltpu.VMEM((depth, width, across), f32)...  75 us

profile of v2, /device:TPU:1, one launch (start us, length us, event | category | flops | bytes accessed | tf_op | source)
XLA Modules:
  0.0 77.7 jit_solution(14396543270286829764)
XLA Ops:
  1.3 75.0 %inversion.1 = (f32[32,64,128]{2,1,0:T(8,128)S(1)}, f32[32,64,128]{2,1,0:T(8,128)S(1)}, f32[32,8,128]{2,1,0:T(8,128)S(1)}) custom-call(s32[1]{0:T(128)S(6)} %copy.13.offset_ref, s32[3]{0:T(128)} %bitcast.16, f32[4]{0:T(128)} %bitcast.17, s32[3,1,128]{2,1,0:T(1,128)} %bitcast.15, f32[4,128]{1,0:T(4,128)} %bitcast.14, f32[32,8,128]{2,1,0:T(8,128)} %courant_ref.1, ...), custom_call_target="tpu_custom_call" | custom-call | tf_op jit(solution)/shard_map/inversion/pallas_call | solution.py:557
  76.3 1.4 %write_out.1 = (f32[32,64,128]{2,1,0:T(8,128)}, f32[32,64,128]{2,1,0:T(8,128)}, f32[32,8,128]{2,1,0:T(8,128)}) custom-call(f32[32,64,128]{2,1,0:T(8,128)S(1)} %get-tuple-element.9.refs_0_, f32[32,64,128]{2,1,0:T(8,128)S(1)} %get-tuple-element.10.refs_1_, f32[32,8,128]{2,1,0:T(8,128)S(1)} %get-tuple-element.11.refs_2_), custom_call_target="tpu_custom_call" | custom-call | tf_op jit(solution)/shard_map/write_out/pallas_call | solution.py:610

commit v3 on v2

--- a/solution.py
+++ b/solution.py
@@ -17,6 +17,7 @@
 HALO = 4
 CHUNK = 4
 BLOCK = 12
+PARTS = 2
 SCALE = 5040.0
 CENTRE = -3.0 * 14350.0
 SIDE = (8064.0, -1008.0, 128.0, -9.0)
@@ -57,7 +58,8 @@
     adjoint_a,
     field_b,
     adjoint_b,
-    pieces,
+    pieces_low,
+    pieces_high,
     laps,
     model,
     imaging,
@@ -84,12 +86,14 @@
     sum_recv,
 ):
     fields = ((field_a, adjoint_a), (field_b, adjoint_b))
+    pieces = (pieces_low, pieces_high)
     shot = lax.axis_index("shot")
     slab = lax.axis_index("gz")
     shots = lax.axis_size("shot")
     slabs = lax.axis_size("gz")
     depth, width, across = field_last.shape
     chunks = depth // CHUNK
+    half = depth // PARTS
     has = (slab > 0, slab < slabs - 1)
     beside = (jnp.maximum(slab - 1, 0), jnp.minimum(slab + 1, slabs - 1))
 
@@ -114,7 +118,8 @@
         loads.append(pltpu.make_async_copy(source, fields[buffer][which].at[pl.ds(HALO, depth)], load_sem.at[i]))
     for i, (source, place) in enumerate(
         (
-            (courant_ref, pieces.at[SPREAD]),
+            (courant_ref.at[pl.ds(0, half)], pieces[0].at[SPREAD]),
+            (courant_ref.at[pl.ds(half, half)], pieces[1].at[SPREAD]),
             (receivers_in, receivers_ref),
             (traces_in, traces_ref),
         )
@@ -135,7 +140,7 @@
     barrier = pltpu.get_barrier_semaphore()
     for dx in range(1, COLS):
         pl.semaphore_signal(barrier, inc=1, device_id={"shot": in_row(dx)}, device_id_type=MESH)
-    for r in (-3, -2, -1, 1, 2, 3):
+    for r in (-3, -1, 1, 3):
         pl.semaphore_signal(barrier, inc=1, device_id={"shot": in_column(r)}, device_id_type=MESH)
     for side in range(2):
 
@@ -144,7 +149,7 @@
             pl.semaphore_signal(barrier, inc=1, device_id={"gz": beside[side]}, device_id_type=MESH)
 
     beside_count = jnp.where(has[0], 1, 0) + jnp.where(has[1], 1, 0)
-    pl.semaphore_wait(barrier, COLS - 1 + 6 + beside_count)
+    pl.semaphore_wait(barrier, COLS - 1 + 4 + beside_count)
 
     def halo(turn, which, side):
         place = HALO if side == 0 else depth
@@ -177,25 +182,25 @@
         def _():
             halo(turn, which, side).wait_send()
 
-    def row_copy(i):
+    def row_copy(i, h):
         return pltpu.make_async_remote_copy(
-            src_ref=courant_ref,
-            dst_ref=pieces.at[(SPREAD + COLS, SPREAD + 2 * COLS, SPAN)[i]],
-            send_sem=row_send.at[i],
-            recv_sem=row_recv.at[i],
-            device_id={"shot": in_column((-1, -2, -extra_row)[i])},
+            src_ref=pieces[h].at[SPREAD + COLS] if i == 1 else courant_ref.at[pl.ds(h * half, half)],
+            dst_ref=pieces[h].at[(SPREAD + COLS, SPREAD + 2 * COLS, SPAN)[i]],
+            send_sem=row_send.at[i, h],
+            recv_sem=row_recv.at[i, h],
+            device_id={"shot": in_column((-1, -1, -extra_row)[i])},
             device_id_type=MESH,
         )
 
-    def piece_copy(dx, r):
+    def piece_copy(dx, r, h):
         target = lax.rem(col + dx, COLS)
         slot = COLS * r + col - target + SPREAD
         held = jnp.where((r >= 0) & (r <= 2), SPREAD + COLS * r, SPAN)
         return pltpu.make_async_remote_copy(
-            src_ref=pieces.at[held],
-            dst_ref=pieces.at[slot],
-            send_sem=piece_send.at[dx - 1, r - slab_row(dx)],
-            recv_sem=piece_recv.at[slot],
+            src_ref=pieces[h].at[held],
+            dst_ref=pieces[h].at[slot],
+            send_sem=piece_send.at[dx - 1, r - slab_row(dx), h],
+            recv_sem=piece_recv.at[slot, h],
             device_id={"shot": in_row(dx)},
             device_id_type=MESH,
         )
@@ -203,89 +208,99 @@
     def slab_row(dx):
         return first_row(lax.rem(col + dx, COLS), COLS - dx)
 
-    def piece_arrived(j):
-        pltpu.make_async_copy(pieces.at[j], pieces.at[j], piece_recv.at[j]).wait()
-
-    def part_copy(dx, r):
+    def pieces_arrived(h):
+        for j in range(SPAN):
+            if j % COLS != SPREAD:
+                pltpu.make_async_copy(pieces[h].at[j], pieces[h].at[j], piece_recv.at[j, h]).wait()
+
+    def part_copy(dx, r, h):
         target = lax.rem(col + dx, COLS)
+        at = r - first_row(col, dx)
         return pltpu.make_async_remote_copy(
-            src_ref=outgoing.at[COLS * r + target - col + SPREAD],
-            dst_ref=from_row.at[dx - 1, r - first_row(col, dx)],
-            send_sem=back_send.at[dx - 1, r - first_row(col, dx)],
-            recv_sem=back_recv.at[dx - 1, r - first_row(col, dx)],
+            src_ref=outgoing.at[COLS * r + target - col + SPREAD, pl.ds(h * half, half)],
+            dst_ref=from_row.at[dx - 1, at, pl.ds(h * half, half)],
+            send_sem=back_send.at[dx - 1, at, h],
+            recv_sem=back_recv.at[dx - 1, at, h],
             device_id={"shot": in_row(dx)},
             device_id_type=MESH,
         )
 
-    def part_start(dx, r):
-        first = first_row(col, dx)
-
-        @pl.when((r >= first) & (r <= first + 2))
-        def _():
-            part_copy(dx, r).start()
+    def parts_start(r, h):
+        for dx in (1, 3, 2):
+            first = first_row(col, dx)
+
+            @pl.when((r >= first) & (r <= first + 2))
+            def _():
+                part_copy(dx, r, h).start()
 
     def source_row(dx):
         return first_row(lax.rem(col - dx + COLS, COLS), dx)
 
-    def part_arrived(dx, r):
-        first = source_row(dx)
-
-        @pl.when((r >= first) & (r <= first + 2))
-        def _():
-            place = from_row.at[dx - 1, r - first]
-            pltpu.make_async_copy(place, place, back_recv.at[dx - 1, r - first]).wait()
-
-    def summed(r, own, c):
-        place = pl.ds(pl.multiple_of(c * CHUNK, CHUNK), CHUNK)
+    def parts_arrived(r, h):
+        for dx in range(1, COLS):
+            first = source_row(dx)
+
+            @pl.when((r >= first) & (r <= first + 2))
+            def _():
+                place = from_row.at[dx - 1, r - first, pl.ds(h * half, half)]
+                pltpu.make_async_copy(place, place, back_recv.at[dx - 1, r - first, h]).wait()
+
+    def summed(r, own, place):
         total = outgoing[SPREAD + COLS * r, place] if own else jnp.zeros((CHUNK, WB, across), jnp.float32)
         for dx in range(1, COLS):
             at = r - source_row(dx)
             total = total + from_row[dx - 1, jnp.where((at >= 0) & (at <= 2), at, 3), place]
         return total
 
-    def sum_copy(i):
+    def sum_copy(i, h):
         return pltpu.make_async_remote_copy(
-            src_ref=sums.at[i],
-            dst_ref=from_rows.at[i],
-            send_sem=sum_send.at[i],
-            recv_sem=sum_recv.at[i],
-            device_id={"shot": in_column((1, 2, extra_row)[i])},
+            src_ref=sums.at[i, pl.ds(h * half, half)],
+            dst_ref=from_rows.at[i, pl.ds(h * half, half)],
+            send_sem=sum_send.at[i, h],
+            recv_sem=sum_recv.at[i, h],
+            device_id={"shot": in_column((1, 1, extra_row)[i])},
             device_id_type=MESH,
         )
 
-    def sum_start(i):
+    def over_half(h, body):
+        def turn(c, _):
+            body(pl.ds(pl.multiple_of(c * CHUNK, CHUNK), CHUNK))
+            return 0
+
+        count = half // CHUNK
+        lax.fori_loop(h * count, (h + 1) * count, turn, 0)
+
+    def sum_start(i, h):
         r = (1, 2, extra_row)[i]
-        for dx in range(1, COLS):
-            part_arrived(dx, r)
-
-        def turn(c, _):
-            sums[i, pl.ds(pl.multiple_of(c * CHUNK, CHUNK), CHUNK)] = summed(r, i < 2, c)
-            return 0
-
-        lax.fori_loop(0, chunks, turn, 0)
-        sum_copy(i).start()
-
-    for which in range(2):
-        for side in range(2):
-            halo_start(0, which, side)
-    row_copy(0).start()
-
-    @pl.when(has_extra)
-    def _():
-        row_copy(2).start()
-
-    row_copy(1).start()
-    own_slab = loads.pop(4)
-    own_slab.wait()
-    for dx in range(1, COLS):
-
-        @pl.when(slab_row(dx) <= 0)
-        def _():
-            piece_copy(dx, 0).start()
-
+        parts_arrived(r, h)
+        if i == 0:
+            sum_copy(1, h).wait_recv()
+
+        def body(place):
+            total = summed(r, i < 2, place)
+            sums[i, place] = total + from_rows[1, place] if i == 0 else total
+
+        over_half(h, body)
+        sum_copy(i, h).start()
+
+    def rows_start(h):
+        row_copy(0, h).start()
+
+        @pl.when(has_extra)
+        def _():
+            row_copy(2, h).start()
+
+    rows_start(0)
+    for h in range(PARTS):
+        loads[4 + h].wait()
+        for dx in (1, 3, 2):
+
+            @pl.when(slab_row(dx) <= 0)
+            def _():
+                piece_copy(dx, 0, h).start()
 
     offset = offset_ref[0]
-    for copy in loads[4:]:
+    for copy in loads[6:]:
         copy.wait()
     by_y = banded(2 * across, across, across)
     by_x = banded(width, 2 * width, width)
@@ -409,123 +424,150 @@
 
         laplace(fields[step % 2][which], starts, planes, use)
 
-    def inner(body):
+    def inner(body, first=0, last=(depth - 2 * HALO) // BLOCK):
         def turn(c, _):
             body([pl.multiple_of(c * BLOCK + HALO, CHUNK)], BLOCK)
             return 0
 
-        lax.fori_loop(0, (depth - 2 * HALO) // BLOCK, turn, 0)
-
-    def pass_on_near():
-        row_copy(0).wait_recv()
+        lax.fori_loop(first, last, turn, 0)
+
+    def pass_on_near(h):
+        row_copy(0, h).wait_recv()
+        row_copy(1, h).start()
         for dx in (1, 3, 2):
-            piece_copy(dx, 1).start()
+            piece_copy(dx, 1, h).start()
 
         @pl.when(has_extra)
         def _():
-            row_copy(2).wait_recv()
+            row_copy(2, h).wait_recv()
 
         for dx in range(1, COLS):
             first = slab_row(dx)
 
             @pl.when(first != 0)
             def _():
-                piece_copy(dx, jnp.where(first < 0, -1, 3)).start()
-
-    def pass_on_later():
-        row_copy(1).wait_recv()
-        for dx in range(1, COLS):
+                piece_copy(dx, jnp.where(first < 0, -1, 3), h).start()
+
+    def pass_on_later(h):
+        row_copy(1, h).wait_recv()
+        for dx in (1, 3, 2):
 
             @pl.when(slab_row(dx) >= 0)
             def _():
-                piece_copy(dx, 2).start()
+                piece_copy(dx, 2, h).start()
+
+    def build_model(h):
+        pieces_arrived(h)
+        for s in range(WB):
+            model[pl.ds(h * half, half), pl.ds(s * WB, WB), :] = pieces[h][offset + SPREAD + s] * (1.0 / SCALE)
 
     ends = (0, depth - CHUNK)
     for copy in loads[:2]:
         copy.wait()
     inner(functools.partial(first_part, 0))
-    pass_on_near()
+    row_copy(0, 0).wait_send()
+    rows_start(1)
     inner(functools.partial(first_part, 1))
+    for h in range(PARTS):
+        pass_on_near(h)
+    for h in range(PARTS):
+        pass_on_later(h)
+    for which in range(2):
+        for side in range(2):
+            halo_start(0, which, side)
+    for copy in loads[2:4]:
+        copy.wait()
+    build_model(0)
+    for which in range(2):
+        inner(functools.partial(second_part, which), 0, 1)
     for which in range(2):
         for side in range(2):
             halo_arrived(0, which, side)
         first_part(which, ends, CHUNK)
-    for copy in loads[2:4]:
-        copy.wait()
-    pass_on_later()
-    for j in range(SPAN):
-        if j % COLS != SPREAD:
-            piece_arrived(j)
-    for s in range(WB):
-        model[:, s * WB : (s + 1) * WB, :] = pieces[offset + SPREAD + s] * (1.0 / SCALE)
+    build_model(1)
     for which in range(2):
         second_part(which, ends, CHUNK)
         for side in range(2):
             halo_start(1, which, side)
     for which in range(2):
-        inner(functools.partial(second_part, which))
-
+        inner(functools.partial(second_part, which), 1)
+
+    def image_out(h):
+        place = pl.ds(h * half, half)
+        for j in range(SPAN):
+            outgoing[j, place] = shown[j + 2 - offset, place]
+        for r in (2, -1, 3):
+            parts_start(r, h)
+
+    from_row[:, 3] = jnp.zeros((COLS - 1, depth, WB, across), jnp.float32)
     for step in range(1, STEPS):
         for which in range(2):
+            body = functools.partial(whole, step, which)
             for side in range(2):
                 halo_arrived(step, which, side)
                 if step > 1:
                     halo_sent(step - 1, which, side)
-            whole(step, which, ends, CHUNK)
+            body(ends, CHUNK)
             if step < STEPS - 1:
                 for side in range(2):
                     halo_start(step + 1, which, side)
-            inner(functools.partial(whole, step, which))
-            if step == STEPS - 1 and which == 0:
-                for j in range(SPAN):
-                    outgoing[j] = shown[j + 2 - offset]
-                for r in (2, -1, 3, 1, 0):
-                    for dx in (1, 3, 2):
-                        part_start(dx, r)
-                from_row[:, 3] = jnp.zeros((COLS - 1, depth, WB, across), jnp.float32)
-    sum_start(1)
-
-    @pl.when(has_extra)
-    def _():
-        sum_start(2)
-
-    sum_start(0)
-    for dx in range(1, COLS):
-        part_arrived(dx, 0)
-    for i in (0, 1):
-        sum_copy(i).wait_recv()
-
-    @pl.when(has_extra)
-    def _():
-        sum_copy(2).wait_recv()
+                inner(body)
+            elif which == 0:
+                inner(body, 0, 1)
+                image_out(0)
+                inner(body, 1)
+                image_out(1)
+            else:
+                for h in range(PARTS):
+                    parts_start(1, h)
+                inner(body)
+    for h in range(PARTS):
+        sum_start(1, h)
+
+        @pl.when(has_extra)
+        def _():
+            sum_start(2, h)
+
+        parts_start(0, h)
+    for h in range(PARTS):
+        sum_start(0, h)
 
     @pl.when(jnp.logical_not(has_extra))
     def _():
         from_rows[2] = jnp.zeros((depth, WB, across), jnp.float32)
 
-    def add_up(c, _):
-        place = pl.ds(pl.multiple_of(c * CHUNK, CHUNK), CHUNK)
-        gradient_out[place] = summed(0, True, c) + from_rows[0, place] + from_rows[1, place] + from_rows[2, place]
-        return 0
-
-    lax.fori_loop(0, chunks, add_up, 0)
+    for h in range(PARTS):
+        parts_arrived(0, h)
+        sum_copy(0, h).wait_recv()
+
+        @pl.when(has_extra)
+        def _():
+            sum_copy(2, h).wait_recv()
+
+        def add_up(place):
+            gradient_out[place] = summed(0, True, place) + from_rows[0, place] + from_rows[2, place]
+
+        over_half(h, add_up)
     for which in range(2):
         for side in range(2):
             halo_sent(0, which, side)
             halo_sent(STEPS - 1, which, side)
-    for i in (0, 1):
-        row_copy(i).wait_send()
-        sum_copy(i).wait_send()
-
-    @pl.when(has_extra)
-    def _():
-        row_copy(2).wait_send()
-        sum_copy(2).wait_send()
-
-    for dx in range(1, COLS):
-        for t in range(3):
-            piece_copy(dx, slab_row(dx) + t).wait_send()
-            part_copy(dx, first_row(col, dx) + t).wait_send()
+    for h in range(PARTS):
+        if h > 0:
+            row_copy(0, h).wait_send()
+        row_copy(1, h).wait_send()
+        for i in (0, 1):
+            sum_copy(i, h).wait_send()
+
+        @pl.when(has_extra)
+        def _():
+            row_copy(2, h).wait_send()
+            sum_copy(2, h).wait_send()
+
+        for dx in range(1, COLS):
+            for t in range(3):
+                piece_copy(dx, slab_row(dx) + t, h).wait_send()
+                part_copy(dx, first_row(col, dx) + t, h).wait_send()
 
 
 def write_out(*refs):
@@ -565,7 +607,7 @@
         out_specs=(vmem, vmem, vmem),
         scratch_shapes=[
             *[pltpu.VMEM((depth + 2 * HALO, width, across), f32)] * 4,
-            pltpu.VMEM((SPAN + 1, depth, WB, across), f32),
+            *[pltpu.VMEM((SPAN + 1, depth // PARTS, WB, across), f32)] * PARTS,
             pltpu.VMEM((2, depth, width, across), f32),
             pltpu.VMEM((depth, width, across), f32),
             pltpu.VMEM((depth, width, across), f32),
@@ -579,17 +621,17 @@
             pltpu.VMEM((width, across), f32),
             pltpu.VMEM((depth * width, across), jnp.bfloat16),
             pltpu.VMEM((STEPS, across, 2 * across), jnp.bfloat16),
-            dma((7,)),
+            dma((8,)),
             dma((STEPS, 2, 2)),
             dma((STEPS, 2, 2)),
-            dma((3,)),
-            dma((3,)),
-            dma((COLS - 1, 3)),
-            dma((SPAN,)),
-            dma((COLS - 1, 3)),
-            dma((COLS - 1, 3)),
-            dma((3,)),
-            dma((3,)),
+            dma((3, PARTS)),
+            dma((3, PARTS)),
+            dma((COLS - 1, 3, PARTS)),
+            dma((SPAN, PARTS)),
+            dma((COLS - 1, 3, PARTS)),
+            dma((COLS - 1, 3, PARTS)),
+            dma((3, PARTS)),
+            dma((3, PARTS)),
         ],
         compiler_params=pltpu.CompilerParams(
             collective_id=0, has_side_effects=True, vmem_limit_bytes=56 * 1024 * 1024

time: 77.8 us -> 71.1 us (0.914)
  Pallas kernels: 76.4 us -> 69.8 us
    pallas_call x1, Pallas kernels: 75 us -> 68.4 us  [per_device(): pl.pallas_call(kernel, out_shape=(pltpu.VMEM((depth, width, across), f32)...]
where the time goes in v3:
time: 71.1 us; the launch traced here: 71 us
  Pallas kernels  69.8 us (98%)
  between operations  1.29 us (2%)
    pallas_call x1, Pallas kernels, per_device(): pl.pallas_call(kernel, out_shape=(pltpu.VMEM((depth, width, across), f32)...  68.4 us

profile of v3, /device:TPU:1, one launch (start us, length us, event | category | flops | bytes accessed | tf_op | source)
XLA Modules:
  0.0 71.0 jit_solution(17950649873533256397)
XLA Ops:
  1.3 68.4 %inversion.1 = (f32[32,64,128]{2,1,0:T(8,128)S(1)}, f32[32,64,128]{2,1,0:T(8,128)S(1)}, f32[32,8,128]{2,1,0:T(8,128)S(1)}) custom-call(s32[1]{0:T(128)S(6)} %copy.13.offset_ref, s32[3]{0:T(128)} %bitcast.16, f32[4]{0:T(128)} %bitcast.17, s32[3,1,128]{2,1,0:T(1,128)} %bitcast.15, f32[4,128]{1,0:T(4,128)} %bitcast.14, f32[32,8,128]{2,1,0:T(8,128)} %courant_ref.1, ...), custom_call_target="tpu_custom_call" | custom-call | tf_op jit(solution)/shard_map/inversion/pallas_call | solution.py:599
  69.7 1.4 %write_out.1 = (f32[32,64,128]{2,1,0:T(8,128)}, f32[32,64,128]{2,1,0:T(8,128)}, f32[32,8,128]{2,1,0:T(8,128)}) custom-call(f32[32,64,128]{2,1,0:T(8,128)S(1)} %get-tuple-element.9.refs_0_, f32[32,64,128]{2,1,0:T(8,128)S(1)} %get-tuple-element.10.refs_1_, f32[32,8,128]{2,1,0:T(8,128)S(1)} %get-tuple-element.11.refs_2_), custom_call_target="tpu_custom_call" | custom-call | tf_op jit(solution)/shard_map/write_out/pallas_call | solution.py:652

commit v4 on v3

--- a/solution.py
+++ b/solution.py
@@ -14,6 +14,7 @@
 SPREAD = 2
 STEPS = 4
 SPAN = WB + 2 * SPREAD
+FAR = WB + SPREAD - 1
 HALO = 4
 CHUNK = 4
 BLOCK = 12
@@ -99,8 +100,9 @@
 
     row, col = shot // COLS, lax.rem(shot, COLS)
     rows = shots // COLS
-    has_extra = col != 1
-    extra_row = jnp.where(col == 0, 3, -1)
+    has_extra = col > 1
+    is_far = (col == 0) | (col == COLS - 1)
+    far_shot = lax.rem(jnp.where(col == 0, shot - FAR, shot + FAR) + shots, shots)
 
     def in_row(dx):
         return row * COLS + lax.rem(col + dx, COLS)
@@ -140,8 +142,13 @@
     barrier = pltpu.get_barrier_semaphore()
     for dx in range(1, COLS):
         pl.semaphore_signal(barrier, inc=1, device_id={"shot": in_row(dx)}, device_id_type=MESH)
-    for r in (-3, -1, 1, 3):
+    for r in (-1, 1):
         pl.semaphore_signal(barrier, inc=1, device_id={"shot": in_column(r)}, device_id_type=MESH)
+
+    @pl.when(is_far)
+    def _():
+        pl.semaphore_signal(barrier, inc=1, device_id={"shot": far_shot}, device_id_type=MESH)
+
     for side in range(2):
 
         @pl.when(has[side])
@@ -149,7 +156,7 @@
             pl.semaphore_signal(barrier, inc=1, device_id={"gz": beside[side]}, device_id_type=MESH)
 
     beside_count = jnp.where(has[0], 1, 0) + jnp.where(has[1], 1, 0)
-    pl.semaphore_wait(barrier, COLS - 1 + 4 + beside_count)
+    pl.semaphore_wait(barrier, COLS - 1 + 2 + jnp.where(is_far, 1, 0) + beside_count)
 
     def halo(turn, which, side):
         place = HALO if side == 0 else depth
@@ -188,20 +195,40 @@
             dst_ref=pieces[h].at[(SPREAD + COLS, SPREAD + 2 * COLS, SPAN)[i]],
             send_sem=row_send.at[i, h],
             recv_sem=row_recv.at[i, h],
-            device_id={"shot": in_column((-1, -1, -extra_row)[i])},
+            device_id={"shot": in_column((-1, -1, 1)[i])},
             device_id_type=MESH,
         )
 
     def piece_copy(dx, r, h):
         target = lax.rem(col + dx, COLS)
         slot = COLS * r + col - target + SPREAD
-        held = jnp.where((r >= 0) & (r <= 2), SPREAD + COLS * r, SPAN)
+        held = jnp.where(r >= 0, jnp.minimum(SPREAD + COLS * r, SPAN), SPAN)
         return pltpu.make_async_remote_copy(
             src_ref=pieces[h].at[held],
             dst_ref=pieces[h].at[slot],
             send_sem=piece_send.at[dx - 1, r - slab_row(dx), h],
             recv_sem=piece_recv.at[slot, h],
             device_id={"shot": in_row(dx)},
+            device_id_type=MESH,
+        )
+
+    def far_copy(h):
+        return pltpu.make_async_remote_copy(
+            src_ref=courant_ref.at[pl.ds(h * half, half)],
+            dst_ref=pieces[h].at[SPAN - 1],
+            send_sem=piece_send.at[COLS - 2, 2, h],
+            recv_sem=piece_recv.at[SPAN - 1, h],
+            device_id={"shot": far_shot},
+            device_id_type=MESH,
+        )
+
+    def far_part(h):
+        return pltpu.make_async_remote_copy(
+            src_ref=outgoing.at[SPAN - 1, pl.ds(h * half, half)],
+            dst_ref=from_rows.at[2, pl.ds(h * half, half)],
+            send_sem=back_send.at[0, 2, h],
+            recv_sem=sum_recv.at[2, h],
+            device_id={"shot": far_shot},
             device_id_type=MESH,
         )
 
@@ -258,7 +285,7 @@
             dst_ref=from_rows.at[i, pl.ds(h * half, half)],
             send_sem=sum_send.at[i, h],
             recv_sem=sum_recv.at[i, h],
-            device_id={"shot": in_column((1, 1, extra_row)[i])},
+            device_id={"shot": in_column((1, 1, -1)[i])},
             device_id_type=MESH,
         )
 
@@ -271,7 +298,7 @@
         lax.fori_loop(h * count, (h + 1) * count, turn, 0)
 
     def sum_start(i, h):
-        r = (1, 2, extra_row)[i]
+        r = (1, 2, -1)[i]
         parts_arrived(r, h)
         if i == 0:
             sum_copy(1, h).wait_recv()
@@ -298,6 +325,10 @@
             @pl.when(slab_row(dx) <= 0)
             def _():
                 piece_copy(dx, 0, h).start()
+
+        @pl.when(col == 0)
+        def _():
+            far_copy(h).start()
 
     offset = offset_ref[0]
     for copy in loads[6:]:
@@ -444,9 +475,9 @@
         for dx in range(1, COLS):
             first = slab_row(dx)
 
-            @pl.when(first != 0)
+            @pl.when(first < 0)
             def _():
-                piece_copy(dx, jnp.where(first < 0, -1, 3), h).start()
+                piece_copy(dx, -1, h).start()
 
     def pass_on_later(h):
         row_copy(1, h).wait_recv()
@@ -496,7 +527,7 @@
         place = pl.ds(h * half, half)
         for j in range(SPAN):
             outgoing[j, place] = shown[j + 2 - offset, place]
-        for r in (2, -1, 3):
+        for r in (2, -1):
             parts_start(r, h)
 
     from_row[:, 3] = jnp.zeros((COLS - 1, depth, WB, across), jnp.float32)
@@ -528,11 +559,15 @@
         def _():
             sum_start(2, h)
 
+        @pl.when(col == COLS - 1)
+        def _():
+            far_part(h).start()
+
         parts_start(0, h)
     for h in range(PARTS):
         sum_start(0, h)
 
-    @pl.when(jnp.logical_not(has_extra))
+    @pl.when(col == 1)
     def _():
         from_rows[2] = jnp.zeros((depth, WB, across), jnp.float32)
 
@@ -540,7 +575,7 @@
         parts_arrived(0, h)
         sum_copy(0, h).wait_recv()
 
-        @pl.when(has_extra)
+        @pl.when(col != 1)
         def _():
             sum_copy(2, h).wait_recv()
 

time: 71.1 us -> 69.1 us (0.972)
  Pallas kernels: 69.8 us -> 67.7 us
    pallas_call x1, Pallas kernels: 68.4 us -> 66.3 us  [per_device(): pl.pallas_call(kernel, out_shape=(pltpu.VMEM((depth, width, across), f32)...]
where the time goes in v4:
time: 69.1 us; the launch traced here: 69 us
  Pallas kernels  67.7 us (98%)
  between operations  1.29 us (2%)
    pallas_call x1, Pallas kernels, per_device(): pl.pallas_call(kernel, out_shape=(pltpu.VMEM((depth, width, across), f32)...  66.3 us

profile of v4, /device:TPU:1, one launch (start us, length us, event | category | flops | bytes accessed | tf_op | source)
XLA Modules:
  0.0 69.0 jit_solution(5031539450521790342)
XLA Ops:
  1.3 66.3 %inversion.1 = (f32[32,64,128]{2,1,0:T(8,128)S(1)}, f32[32,64,128]{2,1,0:T(8,128)S(1)}, f32[32,8,128]{2,1,0:T(8,128)S(1)}) custom-call(s32[1]{0:T(128)S(6)} %copy.13.offset_ref, s32[3]{0:T(128)} %bitcast.16, f32[4]{0:T(128)} %bitcast.17, s32[3,1,128]{2,1,0:T(1,128)} %bitcast.15, f32[4,128]{1,0:T(4,128)} %bitcast.14, f32[32,8,128]{2,1,0:T(8,128)} %courant_ref.1, ...), custom_call_target="tpu_custom_call" | custom-call | tf_op jit(solution)/shard_map/inversion/pallas_call | solution.py:634
  67.6 1.4 %write_out.1 = (f32[32,64,128]{2,1,0:T(8,128)}, f32[32,64,128]{2,1,0:T(8,128)}, f32[32,8,128]{2,1,0:T(8,128)}) custom-call(f32[32,64,128]{2,1,0:T(8,128)S(1)} %get-tuple-element.9.refs_0_, f32[32,64,128]{2,1,0:T(8,128)S(1)} %get-tuple-element.10.refs_1_, f32[32,8,128]{2,1,0:T(8,128)S(1)} %get-tuple-element.11.refs_2_), custom_call_target="tpu_custom_call" | custom-call | tf_op jit(solution)/shard_map/write_out/pallas_call | solution.py:687

commit v5 on v4

--- a/solution.py
+++ b/solution.py
@@ -79,6 +79,10 @@
     halo_recv,
     row_send,
     row_recv,
+    far_send,
+    far_recv,
+    relay_send,
+    relay_recv,
     piece_send,
     piece_recv,
     back_send,
@@ -95,6 +99,8 @@
     depth, width, across = field_last.shape
     chunks = depth // CHUNK
     half = depth // PARTS
+    quarter = half // 2
+    stretches = ((0, 0, 0, quarter), (0, depth - quarter, quarter, quarter), (1, quarter, 0, half))
     has = (slab > 0, slab < slabs - 1)
     beside = (jnp.maximum(slab - 1, 0), jnp.minimum(slab + 1, slabs - 1))
 
@@ -120,8 +126,10 @@
         loads.append(pltpu.make_async_copy(source, fields[buffer][which].at[pl.ds(HALO, depth)], load_sem.at[i]))
     for i, (source, place) in enumerate(
         (
-            (courant_ref.at[pl.ds(0, half)], pieces[0].at[SPREAD]),
-            (courant_ref.at[pl.ds(half, half)], pieces[1].at[SPREAD]),
+            *(
+                (courant_ref.at[pl.ds(plane, count)], pieces[h].at[SPREAD, pl.ds(at, count)])
+                for h, plane, at, count in stretches
+            ),
             (receivers_in, receivers_ref),
             (traces_in, traces_ref),
         )
@@ -189,13 +197,34 @@
         def _():
             halo(turn, which, side).wait_send()
 
-    def row_copy(i, h):
+    def own_copy(t, slot, send, recv, target):
+        h, plane, at, count = stretches[t]
         return pltpu.make_async_remote_copy(
-            src_ref=pieces[h].at[SPREAD + COLS] if i == 1 else courant_ref.at[pl.ds(h * half, half)],
-            dst_ref=pieces[h].at[(SPREAD + COLS, SPREAD + 2 * COLS, SPAN)[i]],
-            send_sem=row_send.at[i, h],
-            recv_sem=row_recv.at[i, h],
-            device_id={"shot": in_column((-1, -1, 1)[i])},
+            src_ref=courant_ref.at[pl.ds(plane, count)],
+            dst_ref=pieces[h].at[slot, pl.ds(at, count)],
+            send_sem=send,
+            recv_sem=recv,
+            device_id={"shot": target},
+            device_id_type=MESH,
+        )
+
+    def near_copy(i, t):
+        slot = (SPREAD + COLS, SPAN)[i]
+        return own_copy(t, slot, row_send.at[i, t], row_recv.at[i, t], in_column((-1, 1)[i]))
+
+    def far_copy(t):
+        return own_copy(t, SPAN - 1, far_send.at[t], far_recv.at[t], far_shot)
+
+    def in_part(h):
+        return [t for t in range(len(stretches)) if stretches[t][0] == h]
+
+    def relay_copy(h):
+        return pltpu.make_async_remote_copy(
+            src_ref=pieces[h].at[SPREAD + COLS],
+            dst_ref=pieces[h].at[SPREAD + 2 * COLS],
+            send_sem=relay_send.at[h],
+            recv_sem=relay_recv.at[h],
+            device_id={"shot": in_column(-1)},
             device_id_type=MESH,
         )
 
@@ -212,16 +241,6 @@
             device_id_type=MESH,
         )
 
-    def far_copy(h):
-        return pltpu.make_async_remote_copy(
-            src_ref=courant_ref.at[pl.ds(h * half, half)],
-            dst_ref=pieces[h].at[SPAN - 1],
-            send_sem=piece_send.at[COLS - 2, 2, h],
-            recv_sem=piece_recv.at[SPAN - 1, h],
-            device_id={"shot": far_shot},
-            device_id_type=MESH,
-        )
-
     def far_part(h):
         return pltpu.make_async_remote_copy(
             src_ref=outgoing.at[SPAN - 1, pl.ds(h * half, half)],
@@ -236,9 +255,19 @@
         return first_row(lax.rem(col + dx, COLS), COLS - dx)
 
     def pieces_arrived(h):
-        for j in range(SPAN):
+        for j in range(SPAN - 1):
             if j % COLS != SPREAD:
                 pltpu.make_async_copy(pieces[h].at[j], pieces[h].at[j], piece_recv.at[j, h]).wait()
+
+        @pl.when(col == COLS - 1)
+        def _():
+            for t in in_part(h):
+                far_copy(t).wait_recv()
+
+        @pl.when(col != COLS - 1)
+        def _():
+            j = SPAN - 1
+            pltpu.make_async_copy(pieces[h].at[j], pieces[h].at[j], piece_recv.at[j, h]).wait()
 
     def part_copy(dx, r, h):
         target = lax.rem(col + dx, COLS)
@@ -311,15 +340,18 @@
         sum_copy(i, h).start()
 
     def rows_start(h):
-        row_copy(0, h).start()
+        for t in in_part(h):
+            near_copy(0, t).start()
 
         @pl.when(has_extra)
         def _():
-            row_copy(2, h).start()
+            for t in in_part(h):
+                near_copy(1, t).start()
 
     rows_start(0)
     for h in range(PARTS):
-        loads[4 + h].wait()
+        for t in in_part(h):
+            loads[4 + t].wait()
         for dx in (1, 3, 2):
 
             @pl.when(slab_row(dx) <= 0)
@@ -328,10 +360,11 @@
 
         @pl.when(col == 0)
         def _():
-            far_copy(h).start()
+            for t in in_part(h):
+                far_copy(t).start()
 
     offset = offset_ref[0]
-    for copy in loads[6:]:
+    for copy in loads[7:]:
         copy.wait()
     by_y = banded(2 * across, across, across)
     by_x = banded(width, 2 * width, width)
@@ -463,24 +496,25 @@
         lax.fori_loop(first, last, turn, 0)
 
     def pass_on_near(h):
-        row_copy(0, h).wait_recv()
-        row_copy(1, h).start()
+        for t in in_part(h):
+            near_copy(0, t).wait_recv()
+        relay_copy(h).start()
         for dx in (1, 3, 2):
             piece_copy(dx, 1, h).start()
 
         @pl.when(has_extra)
         def _():
-            row_copy(2, h).wait_recv()
+            for t in in_part(h):
+                near_copy(1, t).wait_recv()
 
         for dx in range(1, COLS):
-            first = slab_row(dx)
-
-            @pl.when(first < 0)
+
+            @pl.when(slab_row(dx) < 0)
             def _():
                 piece_copy(dx, -1, h).start()
 
     def pass_on_later(h):
-        row_copy(1, h).wait_recv()
+        relay_copy(h).wait_recv()
         for dx in (1, 3, 2):
 
             @pl.when(slab_row(dx) >= 0)
@@ -489,39 +523,46 @@
 
     def build_model(h):
         pieces_arrived(h)
-        for s in range(WB):
-            model[pl.ds(h * half, half), pl.ds(s * WB, WB), :] = pieces[h][offset + SPREAD + s] * (1.0 / SCALE)
+        for t in in_part(h):
+            _, plane, at, count = stretches[t]
+            for s in range(WB):
+                found = pieces[h][offset + SPREAD + s, pl.ds(at, count)]
+                model[pl.ds(plane, count), pl.ds(s * WB, WB), :] = found * (1.0 / SCALE)
+
+    def first_ends(which):
+        for side in range(2):
+            halo_arrived(0, which, side)
+        first_part(which, ends, CHUNK)
 
     ends = (0, depth - CHUNK)
     for copy in loads[:2]:
         copy.wait()
     inner(functools.partial(first_part, 0))
-    row_copy(0, 0).wait_send()
+    for t in in_part(0):
+        near_copy(0, t).wait_send()
     rows_start(1)
+    for side in range(2):
+        halo_start(0, 0, side)
     inner(functools.partial(first_part, 1))
     for h in range(PARTS):
         pass_on_near(h)
+    first_ends(0)
     for h in range(PARTS):
         pass_on_later(h)
-    for which in range(2):
-        for side in range(2):
-            halo_start(0, which, side)
+    for side in range(2):
+        halo_start(0, 1, side)
     for copy in loads[2:4]:
         copy.wait()
     build_model(0)
     for which in range(2):
-        inner(functools.partial(second_part, which), 0, 1)
-    for which in range(2):
-        for side in range(2):
-            halo_arrived(0, which, side)
-        first_part(which, ends, CHUNK)
-    build_model(1)
-    for which in range(2):
+        if which == 1:
+            first_ends(1)
         second_part(which, ends, CHUNK)
         for side in range(2):
             halo_start(1, which, side)
+    build_model(1)
     for which in range(2):
-        inner(functools.partial(second_part, which), 1)
+        inner(functools.partial(second_part, which))
 
     def image_out(h):
         place = pl.ds(h * half, half)
@@ -549,23 +590,26 @@
                 inner(body, 1)
                 image_out(1)
             else:
-                for h in range(PARTS):
-                    parts_start(1, h)
                 inner(body)
+    def last_wave():
+        for h in range(PARTS):
+            parts_start(0, h)
+
+            @pl.when(col == COLS - 1)
+            def _():
+                far_part(h).start()
+
     for h in range(PARTS):
         sum_start(1, h)
+        parts_start(1, h)
 
         @pl.when(has_extra)
         def _():
             sum_start(2, h)
 
-        @pl.when(col == COLS - 1)
-        def _():
-            far_part(h).start()
-
-        parts_start(0, h)
-    for h in range(PARTS):
-        sum_start(0, h)
+    sum_start(0, 0)
+    last_wave()
+    sum_start(0, 1)
 
     @pl.when(col == 1)
     def _():
@@ -587,21 +631,34 @@
         for side in range(2):
             halo_sent(0, which, side)
             halo_sent(STEPS - 1, which, side)
+    for t in range(len(stretches)):
+        if t not in in_part(0):
+            near_copy(0, t).wait_send()
+
+        @pl.when(has_extra)
+        def _():
+            near_copy(1, t).wait_send()
+
+        @pl.when(col == 0)
+        def _():
+            far_copy(t).wait_send()
+
     for h in range(PARTS):
-        if h > 0:
-            row_copy(0, h).wait_send()
-        row_copy(1, h).wait_send()
+        relay_copy(h).wait_send()
         for i in (0, 1):
             sum_copy(i, h).wait_send()
 
         @pl.when(has_extra)
         def _():
-            row_copy(2, h).wait_send()
             sum_copy(2, h).wait_send()
 
         for dx in range(1, COLS):
             for t in range(3):
-                piece_copy(dx, slab_row(dx) + t, h).wait_send()
+
+                @pl.when(slab_row(dx) + t < 3)
+                def _():
+                    piece_copy(dx, slab_row(dx) + t, h).wait_send()
+
                 part_copy(dx, first_row(col, dx) + t, h).wait_send()
 
 
@@ -656,11 +713,15 @@
             pltpu.VMEM((width, across), f32),
             pltpu.VMEM((depth * width, across), jnp.bfloat16),
             pltpu.VMEM((STEPS, across, 2 * across), jnp.bfloat16),
-            dma((8,)),
+            dma((9,)),
             dma((STEPS, 2, 2)),
             dma((STEPS, 2, 2)),
-            dma((3, PARTS)),
-            dma((3, PARTS)),
+            dma((2, 3)),
+            dma((2, 3)),
+            dma((3,)),
+            dma((3,)),
+            dma((PARTS,)),
+            dma((PARTS,)),
             dma((COLS - 1, 3, PARTS)),
             dma((SPAN, PARTS)),
             dma((COLS - 1, 3, PARTS)),

time: 69.1 us -> 67.8 us (0.981)
  Pallas kernels: 67.7 us -> 66.4 us
    pallas_call x1, Pallas kernels: 66.3 us -> 65.1 us  [per_device(): pl.pallas_call(kernel, out_shape=(pltpu.VMEM((depth, width, across), f32)...]
where the time goes in v5:
time: 67.8 us; the launch traced here: 67.7 us
  Pallas kernels  66.4 us (98%)
  between operations  1.29 us (2%)
    pallas_call x1, Pallas kernels, per_device(): pl.pallas_call(kernel, out_shape=(pltpu.VMEM((depth, width, across), f32)...  65.1 us
    pallas_call x1, Pallas kernels, per_device(): pl.pallas_call(write_out, out_shape=tuple((jax.ShapeDtypeStruct(x.shape,...  1.37 us

profile of v5, /device:TPU:1, one launch (start us, length us, event | category | flops | bytes accessed | tf_op | source)
XLA Modules:
  0.0 67.7 jit_solution(15367030578152414180)
XLA Ops:
  1.3 65.1 %inversion.1 = (f32[32,64,128]{2,1,0:T(8,128)S(1)}, f32[32,64,128]{2,1,0:T(8,128)S(1)}, f32[32,8,128]{2,1,0:T(8,128)S(1)}) custom-call(s32[1]{0:T(128)S(6)} %copy.13.offset_ref, s32[3]{0:T(128)} %bitcast.16, f32[4]{0:T(128)} %bitcast.17, s32[3,1,128]{2,1,0:T(1,128)} %bitcast.15, f32[4,128]{1,0:T(4,128)} %bitcast.14, f32[32,8,128]{2,1,0:T(8,128)} %courant_ref.1, ...), custom_call_target="tpu_custom_call" | custom-call | tf_op jit(solution)/shard_map/inversion/pallas_call | solution.py:691
  66.4 1.4 %write_out.1 = (f32[32,64,128]{2,1,0:T(8,128)}, f32[32,64,128]{2,1,0:T(8,128)}, f32[32,8,128]{2,1,0:T(8,128)}) custom-call(f32[32,64,128]{2,1,0:T(8,128)S(1)} %get-tuple-element.9.refs_0_, f32[32,64,128]{2,1,0:T(8,128)S(1)} %get-tuple-element.10.refs_1_, f32[32,8,128]{2,1,0:T(8,128)S(1)} %get-tuple-element.11.refs_2_), custom_call_target="tpu_custom_call" | custom-call | tf_op jit(solution)/shard_map/write_out/pallas_call | solution.py:748
